TPU v7x, 512 devices: a whole 4x8x8 slice. The times are simulated.
512 devices in a mesh: tm: 32 (over y, x), space: 16 (over z, core).
Axes of the slice: x: 4, y: 8, z: 8, core: 2. Of those that a mesh axis runs over, the one named last changes fastest.
Arguments:
- local_term: float32 [32, 512, 512], P('tm', 'space'), may hold values from -2 to 16, as said below
- coupling: float32 [32, 512, 512], P('tm', 'space'), may hold values from -0.25 to 1.2
Outputs:
- sigma: float32 [32, 512, 512], P('tm', 'space')
Inputs may be any that keep to these rules, and one draw needn't show every extreme that they name: local_term[t] is symmetric for every time block t.
All inputs are finite; a program needn't handle non-finite values.
Results may differ from a plain program's by a relative error of at most 0.00014.
Values sent between devices are 32-bit elements; how exact they have to be, the bound alone decides.
No kernel may reach another device: no remote copies, remote signals or barrier semaphores. Data moves between devices by JAX's collectives and lax.ppermute only.
A program may use at most 64 MiB of HBM per device.

v0:
```python
import jax
import jax.numpy as jnp
from jax import lax
from jax.sharding import PartitionSpec as P

HIGH = lax.Precision.HIGHEST


def from_behind(shard, axis, by):
    peers = lax.axis_size(axis)
    pairs = [(i, i + by) for i in range(peers) if 0 <= i + by < peers]
    return lax.ppermute(shard, axis, pairs)


def matmul(left, right):
    return jnp.dot(left, right, precision=HIGH, preferred_element_type=jnp.float32)


def inner_rows(left, right):
    return lax.dot_general(
        left, right, (((0,), (0,)), ((), ())), precision=HIGH, preferred_element_type=jnp.float32
    )


def combine(terms, maps, later_terms, later_maps, owner):
    rows, width = terms.shape

    def accumulate(piece):
        product = matmul(later_terms, piece)
        if later_maps is None:
            return (product,)
        return (product, matmul(later_maps, piece))

    folded = accumulate(lax.all_gather(maps, "space", axis=0, tiled=True))
    weighted = folded[0]
    own_columns = lax.dynamic_slice_in_dim(
        lax.all_gather(maps, "space", axis=0, tiled=True), owner * rows, rows, 1
    )
    congruence = inner_rows(own_columns, lax.all_gather(weighted, "space", axis=0, tiled=True))
    new_terms = terms + congruence
    new_maps = None if later_maps is None else folded[1]
    return (new_terms, new_maps)


def local(local_term, coupling):
    terms = local_term[0]
    maps = coupling[0]
    count_tm = lax.axis_size("tm")
    levels = (count_tm - 1).bit_length()
    owner = lax.axis_index("space")
    for level in range(levels):
        offset = 1 << level
        if level == levels - 1:
            later_terms = from_behind(terms, "tm", -offset)
            later_maps = None
        else:
            later_terms, later_maps = from_behind((terms, maps), "tm", -offset)
        terms, maps = combine(terms, maps, later_terms, later_maps, owner)
    return terms[None]


def solution(mesh):
    placed = (P("tm", "space", None), P("tm", "space", None))
    return jax.shard_map(
        local, mesh=mesh, in_specs=placed, out_specs=P("tm", "space", None), check_vma=False
    )
```

profile of v0, /device:TPU:1, one launch (start us, length us, event | category | flops | bytes accessed | tf_op | source)
XLA Modules:
  0.0 450.1 jit_solution(3637459121479575733)
XLA Ops:
  8.7 4.3 collective-permute-done
  13.0 44.4 %all-gather.30.cloned.1.call-done = f32[1,512,512]{2,1,0:T(8,128)} async-done(((f32[1,32,512]{2,1,0:T(8,128)}), f32[1,512,512]{2,1,0:T(8,128)}) %all-gather.30.cloned.1.call-update) | async-done | bytes 1048592 | tf_op jit(solution)/shard_map/all_gather | solution.py:37
  57.4 2.6 fusion.1
  62.1 3.7 collective-permute-done.1
  65.9 1.3 fusion.3
  67.3 33.0 %all-gather.12.cloned.1.call-done = f32[512,512]{1,0:T(8,128)} async-done(((f32[32,512]{1,0:T(8,128)}), f32[512,512]{1,0:T(8,128)}) %all-gather.12.cloned.1.call-update) | async-done | bytes 1048592 | tf_op jit(solution)/shard_map/all_gather | solution.py:39
  100.3 2.0 convolution_add_fusion.4
  102.2 1.3 collective-permute-start.2
  103.5 39.0 %all-gather.14.cloned.1.call-done = f32[512,512]{1,0:T(8,128)} async-done(((f32[32,512]{1,0:T(8,128)}), f32[512,512]{1,0:T(8,128)}) %all-gather.14.cloned.1.call-update) | async-done | bytes 1048592 | tf_op jit(solution)/shard_map/all_gather | solution.py:37
  142.5 2.6 fusion.16
  147.3 5.2 %collective-permute-done.3 = f32[32,512]{1,0:T(8,128)S(1)} collective-permute-done((f32[32,512]{1,0:T(8,128)S(1)}, f32[32,512]{1,0:T(8,128)S(1)}, u32[]{:S(2)}, u32[]{:S(2)}) %collective-permute-start.3) | collective-permute-done | bytes 65568 | tf_op jit(solution)/shard_map/ppermute | solution.py:12
  152.5 1.3 fusion.17
  153.9 31.5 %all-gather.16.cloned.1.call-done = f32[512,512]{1,0:T(8,128)} async-done(((f32[32,512]{1,0:T(8,128)}), f32[512,512]{1,0:T(8,128)}) %all-gather.16.cloned.1.call-update) | async-done | bytes 1048592 | tf_op jit(solution)/shard_map/all_gather | solution.py:39
  185.4 2.0 convolution_add_fusion.3
  187.4 1.3 collective-permute-start.4
  188.7 38.8 %all-gather.18.cloned.1.call-done = f32[512,512]{1,0:T(8,128)} async-done(((f32[32,512]{1,0:T(8,128)}), f32[512,512]{1,0:T(8,128)}) %all-gather.18.cloned.1.call-update) | async-done | bytes 1048592 | tf_op jit(solution)/shard_map/all_gather | solution.py:37
  227.5 2.6 fusion.18
  232.3 3.7 collective-permute-done.5
  236.0 1.3 fusion.19
  237.4 33.0 %all-gather.20.cloned.1.call-done = f32[512,512]{1,0:T(8,128)} async-done(((f32[32,512]{1,0:T(8,128)}), f32[512,512]{1,0:T(8,128)}) %all-gather.20.cloned.1.call-update) | async-done | bytes 1048592 | tf_op jit(solution)/shard_map/all_gather | solution.py:39
  270.4 2.0 convolution_add_fusion.2
  272.4 1.3 collective-permute-start.6
  273.7 39.0 %all-gather.22.cloned.1.call-done = f32[512,512]{1,0:T(8,128)} async-done(((f32[32,512]{1,0:T(8,128)}), f32[512,512]{1,0:T(8,128)}) %all-gather.22.cloned.1.call-update) | async-done | bytes 1048592 | tf_op jit(solution)/shard_map/all_gather | solution.py:37
  312.6 2.6 fusion.20
  317.4 4.6 %collective-permute-done.7 = f32[32,512]{1,0:T(8,128)S(1)} collective-permute-done((f32[32,512]{1,0:T(8,128)S(1)}, f32[32,512]{1,0:T(8,128)S(1)}, u32[]{:S(2)}, u32[]{:S(2)}) %collective-permute-start.7) | collective-permute-done | bytes 65568 | tf_op jit(solution)/shard_map/ppermute | solution.py:12
  322.0 1.3 fusion.21
  323.4 32.1 %all-gather.24.cloned.1.call-done = f32[512,512]{1,0:T(8,128)} async-done(((f32[32,512]{1,0:T(8,128)}), f32[512,512]{1,0:T(8,128)}) %all-gather.24.cloned.1.call-update) | async-done | bytes 1048592 | tf_op jit(solution)/shard_map/all_gather | solution.py:39
  355.5 2.0 convolution_add_fusion.1
  358.8 39.0 %all-gather.26.cloned.1.call-done = f32[512,512]{1,0:T(8,128)} async-done(((f32[32,512]{1,0:T(8,128)}), f32[512,512]{1,0:T(8,128)}) %all-gather.26.cloned.1.call-update) | async-done | bytes 1048592 | tf_op jit(solution)/shard_map/all_gather | solution.py:37
  397.8 2.6 fusion.22
  400.3 40.2 %all-gather.28.cloned.1.call-done = f32[512,512]{1,0:T(8,128)} async-done(((f32[32,512]{1,0:T(8,128)}), f32[512,512]{1,0:T(8,128)}) %all-gather.28.cloned.1.call-update) | async-done | bytes 1048592 | tf_op jit(solution)/shard_map/all_gather | solution.py:39
  440.6 2.7 fusion
  (48 shorter events, 12.1 us)
Async XLA Ops:
  6.5 0.8 copy-start.8
  6.5 50.8 %all-gather.30.cloned.1.call-start = ((), (), s32[]{:S(2)}) async-start(), calls=%async_computation.9 | async-start | bytes 1114112 | tf_op jit(solution)/shard_map/all_gather | solution.py:37
  7.3 93.0 %all-gather.12.cloned.1.call-start = ((), (), s32[]{:S(2)}) async-start(), calls=%async_computation | async-start | bytes 1114112 | tf_op jit(solution)/shard_map/all_gather | solution.py:39
  7.4 5.6 %collective-permute-start = (f32[32,512]{1,0:T(8,128)S(1)}, f32[32,512]{1,0:T(8,128)S(1)}, u32[]{:S(2)}, u32[]{:S(2)}) collective-permute-start(f32[32,512]{1,0:T(8,128)S(1)} %bitcast.35), channel_id=1, source_target_pairs={{16,0},{32,16},{48,32},{64,48},{80,64},{96,80},{112,96},{128,112},... | collective-permute-start | bytes 196616 | tf_op jit(solution)/shard_map/ppermute | solution.py:12
  57.4 8.5 %copy-start.1 = (f32[1,512,512]{2,1,0:T(8,128)S(1)}, f32[1,512,512]{2,1,0:T(8,128)}, u32[]{:S(2)}) copy-start(f32[1,512,512]{2,1,0:T(8,128)} %all-gather.30.cloned.1.call-done) | copy-start | bytes 3145732
  60.0 0.8 copy-start.7
  60.0 82.5 %all-gather.14.cloned.1.call-start = ((), (), s32[]{:S(2)}) async-start(), calls=%async_computation.1 | async-start | bytes 1114112 | tf_op jit(solution)/shard_map/all_gather | solution.py:37
  60.9 5.0 %collective-permute-start.1 = (f32[32,512]{1,0:T(8,128)S(1)}, f32[32,512]{1,0:T(8,128)S(1)}, u32[]{:S(2)}, u32[]{:S(2)}) collective-permute-start(f32[32,512]{1,0:T(8,128)S(1)} %bitcast.34), channel_id=1, source_target_pairs={{16,0},{32,16},{48,32},{64,48},{80,64},{96,80},{112,96},{128,112},... | collective-permute-start | bytes 196616 | tf_op jit(solution)/shard_map/ppermute | solution.py:12
  67.2 118.2 %all-gather.16.cloned.1.call-start = ((), (), s32[]{:S(2)}) async-start(), calls=%async_computation.2 | async-start | bytes 1114112 | tf_op jit(solution)/shard_map/all_gather | solution.py:39
  102.2 40.3 %collective-permute-start.2 = (f32[32,512]{1,0:T(8,128)S(1)}, f32[32,512]{1,0:T(8,128)S(1)}, u32[]{:S(2)}, u32[]{:S(2)}) collective-permute-start(f32[32,512]{1,0:T(8,128)S(1)} %convolution_add_fusion.4), channel_id=1, source_target_pairs={{32,0},{48,16},{64,32},{80,48},{96,64},{112,80},{128,96},{144,112}... | collective-permute-start | bytes 196616 | tf_op jit(solution)/shard_map/ppermute | solution.py:12
  142.5 10.0 %copy-start = (f32[512,512]{1,0:T(8,128)S(1)}, f32[512,512]{1,0:T(8,128)}, u32[]{:S(2)}) copy-start(f32[512,512]{1,0:T(8,128)} %all-gather.14.cloned.1.call-done) | copy-start | bytes 3145732
  145.2 0.8 copy-start.4
  145.2 82.3 %all-gather.18.cloned.1.call-start = ((), (), s32[]{:S(2)}) async-start(), calls=%async_computation.3 | async-start | bytes 1114112 | tf_op jit(solution)/shard_map/all_gather | solution.py:37
  146.0 6.5 %collective-permute-start.3 = (f32[32,512]{1,0:T(8,128)S(1)}, f32[32,512]{1,0:T(8,128)S(1)}, u32[]{:S(2)}, u32[]{:S(2)}) collective-permute-start(f32[32,512]{1,0:T(8,128)S(1)} %copy-done.4), channel_id=1, source_target_pairs={{32,0},{48,16},{64,32},{80,48},{96,64},{112,80},{128,96},{144,112}... | collective-permute-start | bytes 196616 | tf_op jit(solution)/shard_map/ppermute | solution.py:12
  153.8 116.6 %all-gather.20.cloned.1.call-start = ((), (), s32[]{:S(2)}) async-start(), calls=%async_computation.4 | async-start | bytes 1114112 | tf_op jit(solution)/shard_map/all_gather | solution.py:39
  187.4 40.1 %collective-permute-start.4 = (f32[32,512]{1,0:T(8,128)S(1)}, f32[32,512]{1,0:T(8,128)S(1)}, u32[]{:S(2)}, u32[]{:S(2)}) collective-permute-start(f32[32,512]{1,0:T(8,128)S(1)} %convolution_add_fusion.3), channel_id=1, source_target_pairs={{64,0},{80,16},{96,32},{112,48},{128,64},{144,80},{160,96},{176,11... | collective-permute-start | bytes 196616 | tf_op jit(solution)/shard_map/ppermute | solution.py:12
  227.5 8.5 %copy-start.2 = (f32[512,512]{1,0:T(8,128)S(1)}, f32[512,512]{1,0:T(8,128)}, u32[]{:S(2)}) copy-start(f32[512,512]{1,0:T(8,128)} %all-gather.18.cloned.1.call-done) | copy-start | bytes 3145732
  230.1 0.8 copy-start.5
  230.2 82.5 %all-gather.22.cloned.1.call-start = ((), (), s32[]{:S(2)}) async-start(), calls=%async_computation.5 | async-start | bytes 1114112 | tf_op jit(solution)/shard_map/all_gather | solution.py:37
  231.0 5.0 %collective-permute-start.5 = (f32[32,512]{1,0:T(8,128)S(1)}, f32[32,512]{1,0:T(8,128)S(1)}, u32[]{:S(2)}, u32[]{:S(2)}) collective-permute-start(f32[32,512]{1,0:T(8,128)S(1)} %copy-done.5), channel_id=1, source_target_pairs={{64,0},{80,16},{96,32},{112,48},{128,64},{144,80},{160,96},{176,11... | collective-permute-start | bytes 196616 | tf_op jit(solution)/shard_map/ppermute | solution.py:12
  237.3 118.2 %all-gather.24.cloned.1.call-start = ((), (), s32[]{:S(2)}) async-start(), calls=%async_computation.6 | async-start | bytes 1114112 | tf_op jit(solution)/shard_map/all_gather | solution.py:39
  272.4 40.3 %collective-permute-start.6 = (f32[32,512]{1,0:T(8,128)S(1)}, f32[32,512]{1,0:T(8,128)S(1)}, u32[]{:S(2)}, u32[]{:S(2)}) collective-permute-start(f32[32,512]{1,0:T(8,128)S(1)} %convolution_add_fusion.2), channel_id=1, source_target_pairs={{128,0},{144,16},{160,32},{176,48},{192,64},{208,80},{224,96},{240... | collective-permute-start | bytes 196616 | tf_op jit(solution)/shard_map/ppermute | solution.py:12
  312.6 9.4 %copy-start.3 = (f32[512,512]{1,0:T(8,128)S(1)}, f32[512,512]{1,0:T(8,128)}, u32[]{:S(2)}) copy-start(f32[512,512]{1,0:T(8,128)} %all-gather.22.cloned.1.call-done) | copy-start | bytes 3145732
  315.3 0.8 copy-start.6
  315.3 82.5 %all-gather.26.cloned.1.call-start = ((), (), s32[]{:S(2)}) async-start(), calls=%async_computation.7 | async-start | bytes 1114112 | tf_op jit(solution)/shard_map/all_gather | solution.py:37
  316.1 5.9 %collective-permute-start.7 = (f32[32,512]{1,0:T(8,128)S(1)}, f32[32,512]{1,0:T(8,128)S(1)}, u32[]{:S(2)}, u32[]{:S(2)}) collective-permute-start(f32[32,512]{1,0:T(8,128)S(1)} %copy-done.6), channel_id=1, source_target_pairs={{128,0},{144,16},{160,32},{176,48},{192,64},{208,80},{224,96},{240... | collective-permute-start | bytes 196616 | tf_op jit(solution)/shard_map/ppermute | solution.py:12
  323.4 117.2 %all-gather.28.cloned.1.call-start = ((), (), s32[]{:S(2)}) async-start(), calls=%async_computation.8 | async-start | bytes 1114112 | tf_op jit(solution)/shard_map/all_gather | solution.py:39
  357.5 40.3 %collective-permute-start.8 = (f32[32,512]{1,0:T(8,128)S(1)}, f32[32,512]{1,0:T(8,128)S(1)}, u32[]{:S(2)}, u32[]{:S(2)}) collective-permute-start(f32[32,512]{1,0:T(8,128)S(1)} %convolution_add_fusion.1), channel_id=1, source_target_pairs={{256,0},{272,16},{288,32},{304,48},{320,64},{336,80},{352,96},{368... | collective-permute-start | bytes 196616 | tf_op jit(solution)/shard_map/ppermute | solution.py:12
Sparse Core Ops, SparseCore 0:
  9.5 47.8 all-gather.29
  60.2 40.0 all-gather.11
  102.4 40.0 all-gather.13
  145.3 40.0 all-gather.15
  187.4 40.0 all-gather.17
  230.3 40.0 all-gather.19
  272.5 40.0 all-gather.21
  315.4 40.0 all-gather.23
  357.7 40.0 all-gather.25
  400.5 40.0 all-gather.27
where the time goes:
time: 451 us; the launch traced here: 450 us
  waiting for transfers between devices  392 us (87%)
  matrix products  28.9 us (6%)
  between operations  13.7 us (3%)
  starting transfers between devices  11.9 us (3%)
    all_gather x5, waiting for transfers between devices, combine(): lax.all_gather(maps, 'space', axis=0, tiled=True)  200 us
    all_gather x5, waiting for transfers between devices, combine(): lax.all_gather(weighted, 'space', axis=0, tiled=True)  170 us
    ppermute x9, waiting for transfers between devices, from_behind(): return lax.ppermute(shard, axis, pairs)  21.6 us
    dot_general x9, matrix products, matmul(): jnp.dot(left, right, precision=HIGH, preferred_element_type=jnp.float32)  18.4 us
    ppermute x9, starting transfers between devices, from_behind(): return lax.ppermute(shard, axis, pairs)  11.6 us
    dot_general x5, matrix products, inner_rows(): lax.dot_general(left, right, (((0,), (0,)), ((), ())), precision=HIGH, pr...  10.5 us
  transfers between devices with their start and end apart: 19, of which 15 were waited for; matrix products, arithmetic and copies ran while one was open for 3% of the time, Pallas kernels for 0%

commit v1 on v0

v1 whole, which is shorter than its diff:
```python
import functools

import jax
import jax.numpy as jnp
import numpy as np
from jax import lax
from jax.experimental import pallas as pl
from jax.experimental.pallas import tpu as pltpu
from jax.sharding import Mesh, PartitionSpec as P

AXES = ("yh", "yl", "x", "z", "core")
SIZES = (4, 2, 4, 8, 2)
GROUP = ("yl", "x")
BLOCKS = 32
RADICES = (2, 2, 2, 2, 2)


def site(block):
    return (block % 32) // 8, block % 8


def origin(block, rows):
    return (block % 32) * 16 + rows


def place(block, rows):
    yh, z = site(block)
    core, chip = divmod(rows, 8)
    return int(np.ravel_multi_index((yh, chip // 4, chip % 4, z, core), SIZES))


def move(array, source, target):
    pairs = [(source(t, r), target(t, r)) for t in range(BLOCKS) for r in range(16)]
    return lax.ppermute(array, AXES, pairs)


def split(x):
    high = x.astype(jnp.bfloat16)
    return high, (x - high.astype(jnp.float32)).astype(jnp.bfloat16)


def product(left, right, transposed=False):
    dims = (((1,), (1 if transposed else 0,)), ((), ()))
    high, low = left
    rows = high.shape[0]
    dot = functools.partial(lax.dot_general, dimension_numbers=dims, preferred_element_type=jnp.float32)
    both = dot(jnp.concatenate([high, low], 0), right[0])
    return both[:rows] + both[rows:] + dot(high, right[1])


def combine_kernel(radix, last, info, mine, theirs, first_term, last_map, out, turned):
    core, column = info[0], info[1]

    def halves(slot):
        return [split(half[:, slot].reshape(256, 512)) for half in (mine, theirs)]

    def times(left, right):
        pieces = [product(split(left[:, 256 * i : 256 * i + 256]), right[i]) for i in range(2)]
        return pieces[0] + pieces[1]

    def times_turned(left, right):
        parts = split(left)
        return jnp.concatenate([product(parts, right[i], True) for i in range(2)], 1)

    def ordered(rows):
        return jnp.where(core == 0, rows, jnp.concatenate([rows[:, 256:], rows[:, :256]], 1))

    slab = pl.ds(pl.multiple_of((column // 4) * 128, 128), 128)
    for i, half in enumerate((mine, theirs)):
        turned[:, 256 * i : 256 * i + 256] = half[:, 0, :, slab].reshape(256, 128).T
    left = turned[pl.ds(pl.multiple_of((column % 4) * 32, 32), 32), :]

    maps = [halves(i) for i in range(radix - 1)]
    weighted = []
    for i in range(1, radix):
        weighted.append(times(left, halves(radix - 2 + i)))
        if i < radix - 1:
            left = times_turned(left, maps[i])
    total = None
    chain = last_map[...]
    for i in reversed(range(radix - 1)):
        here = weighted[i] if total is None else weighted[i] + total
        if last:
            total = times(ordered(here), maps[i])
        else:
            both = times(ordered(jnp.concatenate([here, chain], 0)), maps[i])
            total, chain = both[:32], both[32:]
        total = jnp.where(info[2 + i] != 0, total, 0.0)
    term = first_term[...] + total
    if last:
        out[...] = term
    else:
        out[0] = chain
        out[1] = term


def combine(radix, last, info, mine, theirs, first_term, last_map):
    vmem = pl.BlockSpec(memory_space=pltpu.VMEM)
    shape = (32, 512) if last else (2, 32, 512)
    return pl.pallas_call(
        functools.partial(combine_kernel, radix, last),
        out_shape=jax.ShapeDtypeStruct(shape, jnp.float32),
        in_specs=[pl.BlockSpec(memory_space=pltpu.SMEM)] + [vmem] * 4,
        out_specs=vmem,
        scratch_shapes=[pltpu.VMEM((128, 512), jnp.float32)],
        compiler_params=pltpu.CompilerParams(vmem_limit_bytes=48 * 1024 * 1024),
    )(info, mine, theirs, first_term, last_map)


def local(local_term, coupling):
    core = lax.axis_index("core")
    column = core * 8 + lax.axis_index(GROUP)
    end = lax.axis_index("yh") * 8 + lax.axis_index("z")
    both = jnp.concatenate([coupling, local_term], 0)
    length = 1
    for stage, radix in enumerate(RADICES):
        last = stage == len(RADICES) - 1
        if stage == 0:
            windows = [
                move(both, origin, lambda t, r, d=d: place(t + d, r)) for d in reversed(range(radix))
            ]
        else:
            windows = [
                move(both, place, lambda t, r, d=d: place(t + d * length, r)) for d in reversed(range(1, radix))
            ] + [both]
        rows = jnp.stack([w[0] for w in windows[:-1]] + [w[1] for w in windows[1:]])
        mine = lax.all_to_all(jnp.broadcast_to(rows[None], (8,) + rows.shape), GROUP, 0, 0, tiled=True)
        theirs = lax.ppermute(mine, "core", [(0, 1), (1, 0)])
        begin = (end - radix * length + 1) % BLOCKS
        counts = [(begin + i * length < BLOCKS).astype(jnp.int32) for i in range(1, radix)]
        info = jnp.stack([core, column] + counts).astype(jnp.int32)
        both = combine(radix, last, info, mine, theirs, windows[0][1], windows[-1][0])
        length *= radix
    return move(both, lambda t, r: place(t + BLOCKS - 1, r), origin)[None]


def solution(mesh):
    fine = Mesh(mesh.devices.reshape(SIZES), AXES)
    spec = P(("yh", "yl", "x"), ("z", "core"), None)
    return jax.shard_map(local, mesh=fine, in_specs=(spec, spec), out_specs=spec, check_vma=False)
```

time: 451 us -> 225 us (0.50)
  waiting for transfers between devices: 392 us -> 80.9 us
  blocking collectives: 0 us -> 88.2 us
  starting transfers between devices: 11.9 us -> 45.2 us
  matrix products: 28.9 us -> 0 us
  between operations: 13.7 us -> 0.38 us
  Pallas kernels: 0 us -> 6.22 us
    all_gather x10 -> x0, waiting for transfers between devices: 370 us -> none  [the longest x5 200 us: combine(): lax.all_gather(maps, 'space', axis=0, tiled=True)]
    all_to_all x0 -> x5, blocking collectives: none -> 88.2 us  [local(): lax.all_to_all(jnp.broadcast_to(rows[None], (8,) + rows.shape), GROUP, 0,...]
    ppermute x9 -> x12, waiting for transfers between devices: 21.6 us -> 80.9 us  [the longest x7 69.9 us: move(): return lax.ppermute(array, AXES, pairs)]
    ppermute x9 -> x12, starting transfers between devices: 11.6 us -> 45.2 us  [the longest x7 22.7 us: move(): return lax.ppermute(array, AXES, pairs)]
    dot_general x14 -> x0, matrix products: 28.9 us -> none  [the longest x9 18.4 us: matmul(): jnp.dot(left, right, precision=HIGH, preferred_element_type=jnp.float32)]
    pallas_call x0 -> x5, Pallas kernels: none -> 6.22 us  [combine(): pl.pallas_call(functools.partial(combine_kernel, radix, last), out_shape=...]
  transfers between devices with their start and end apart: 19 -> 12, of which waited for: 15 -> 12; matrix products, arithmetic and copies ran while one was open for 3% -> 0% of each run, Pallas kernels for 0% -> 0%
where the time goes in v1:
time: 225 us; the launch traced here: 223 us
  blocking collectives  88.2 us (39%)
  waiting for transfers between devices  80.9 us (36%)
  starting transfers between devices  45.2 us (20%)
  Pallas kernels  6.22 us (3%)
    all_to_all x5, blocking collectives, local(): lax.all_to_all(jnp.broadcast_to(rows[None], (8,) + rows.shape), GROUP, 0,...  88.2 us
    ppermute x7, waiting for transfers between devices, move(): return lax.ppermute(array, AXES, pairs)  69.9 us
    ppermute x7, starting transfers between devices, move(): return lax.ppermute(array, AXES, pairs)  22.7 us
    ppermute x5, starting transfers between devices, local(): theirs = lax.ppermute(mine, 'core', [(0, 1), (1, 0)])  22.5 us
    ppermute x5, waiting for transfers between devices, local(): theirs = lax.ppermute(mine, 'core', [(0, 1), (1, 0)])  11.1 us
    pallas_call x5, Pallas kernels, combine(): pl.pallas_call(functools.partial(combine_kernel, radix, last), out_shape=...  6.22 us
  transfers between devices with their start and end apart: 12, of which 12 were waited for; matrix products, arithmetic and copies ran while one was open for 0% of the time, Pallas kernels for 0%

profile of v1, /device:TPU:1, one launch (start us, length us, event | category | flops | bytes accessed | tf_op | source)
XLA Modules:
  0.0 223.3 jit_solution(14620680837256724492)
XLA Ops:
  0.9 4.5 %collective-permute-start.1 = (f32[2,32,512]{2,1,0:T(8,128)S(1)}, f32[2,32,512]{2,1,0:T(8,128)S(1)}, u32[]{:S(2)}, u32[]{:S(2)}) collective-permute-start(f32[2,32,512]{2,1,0:T(8,128)S(1)} %constant_dynamic-update-slice_fusion), channel_id=1, source_target_pairs={{0,0},{1,16},{2,32},{3,48},{4,64},{5,80},{6,96},{7,112},{8,1},{9,1... | collective-permute-start | bytes 393224 | tf_op jit(solution)/shard_map/ppermute | solution.py:34
  5.4 5.2 %collective-permute-start = (f32[2,32,512]{2,1,0:T(8,128)S(1)}, f32[2,32,512]{2,1,0:T(8,128)S(1)}, u32[]{:S(2)}, u32[]{:S(2)}) collective-permute-start(f32[2,32,512]{2,1,0:T(8,128)S(1)} %constant_dynamic-update-slice_fusion), channel_id=1, source_target_pairs={{0,2},{1,18},{2,34},{3,50},{4,66},{5,82},{6,98},{7,114},{8,3},{9,1... | collective-permute-start | bytes 393224 | tf_op jit(solution)/shard_map/ppermute | solution.py:34
  10.6 5.6 %collective-permute-done.1 = f32[2,32,512]{2,1,0:T(8,128)S(1)} collective-permute-done((f32[2,32,512]{2,1,0:T(8,128)S(1)}, f32[2,32,512]{2,1,0:T(8,128)S(1)}, u32[]{:S(2)}, u32[]{:S(2)}) %collective-permute-start.1) | collective-permute-done | bytes 131104 | tf_op jit(solution)/shard_map/ppermute | solution.py:34
  16.2 13.2 %collective-permute-done = f32[2,32,512]{2,1,0:T(8,128)S(1)} collective-permute-done((f32[2,32,512]{2,1,0:T(8,128)S(1)}, f32[2,32,512]{2,1,0:T(8,128)S(1)}, u32[]{:S(2)}, u32[]{:S(2)}) %collective-permute-start) | collective-permute-done | bytes 131104 | tf_op jit(solution)/shard_map/ppermute | solution.py:34
  29.6 17.1 %all_to_all.25.mine = f32[8,2,32,512]{3,2,1,0:T(8,128)S(1)} all-to-all(f32[8,2,32,512]{3,2,1,0:T(8,128)S(1)} %broadcast_in_dim.12), channel_id=1, replica_groups=mesh['yh'=4,'yl'=2,'x'=4,'z'=8,'core'=2] {'yl','x'}, dimensions={0} | all-to-all | bytes 2097152 | tf_op jit(solution)/shard_map/all_to_all | solution.py:127
  46.7 4.9 %collective-permute-start.2 = (f32[8,2,32,512]{3,2,1,0:T(8,128)S(1)}, f32[8,2,32,512]{3,2,1,0:T(8,128)S(1)}, u32[]{:S(2)}, u32[]{:S(2)}) collective-permute-start(f32[8,2,32,512]{3,2,1,0:T(8,128)S(1)} %all_to_all.25.mine), channel_id=1, source_target_pairs={{0,1},{1,0},{2,3},{3,2},{4,5},{5,4},{6,7},{7,6},{8,9},{9,8},{10,11... | collective-permute-start | bytes 3145736 | tf_op jit(solution)/shard_map/ppermute | solution.py:128
  51.8 2.2 collective-permute-done.2.theirs
  55.2 1.9 collective-permute-start.3
  57.1 12.1 %collective-permute-done.3 = f32[2,32,512]{2,1,0:T(8,128)S(1)} collective-permute-done((f32[2,32,512]{2,1,0:T(8,128)S(1)}, f32[2,32,512]{2,1,0:T(8,128)S(1)}, u32[]{:S(2)}, u32[]{:S(2)}) %collective-permute-start.3) | collective-permute-done | bytes 131104 | tf_op jit(solution)/shard_map/ppermute | solution.py:34
  69.3 18.6 %all_to_all.26.mine = f32[8,2,32,512]{3,2,1,0:T(8,128)S(1)} all-to-all(f32[8,2,32,512]{3,2,1,0:T(8,128)S(1)} %broadcast_in_dim.13), channel_id=1, replica_groups=mesh['yh'=4,'yl'=2,'x'=4,'z'=8,'core'=2] {'yl','x'}, dimensions={0} | all-to-all | bytes 2097152 | tf_op jit(solution)/shard_map/all_to_all | solution.py:127
  87.9 4.7 %collective-permute-start.4 = (f32[8,2,32,512]{3,2,1,0:T(8,128)S(1)}, f32[8,2,32,512]{3,2,1,0:T(8,128)S(1)}, u32[]{:S(2)}, u32[]{:S(2)}) collective-permute-start(f32[8,2,32,512]{3,2,1,0:T(8,128)S(1)} %all_to_all.26.mine), channel_id=1, source_target_pairs={{0,1},{1,0},{2,3},{3,2},{4,5},{5,4},{6,7},{7,6},{8,9},{9,8},{10,11... | collective-permute-start | bytes 3145736 | tf_op jit(solution)/shard_map/ppermute | solution.py:128
  92.8 2.1 collective-permute-done.4.theirs
  94.9 1.2 shard_map.29
  96.2 1.9 collective-permute-start.5
  98.1 11.6 %collective-permute-done.5 = f32[2,32,512]{2,1,0:T(8,128)S(1)} collective-permute-done((f32[2,32,512]{2,1,0:T(8,128)S(1)}, f32[2,32,512]{2,1,0:T(8,128)S(1)}, u32[]{:S(2)}, u32[]{:S(2)}) %collective-permute-start.5) | collective-permute-done | bytes 131104 | tf_op jit(solution)/shard_map/ppermute | solution.py:34
  109.9 19.0 %all_to_all.27.mine = f32[8,2,32,512]{3,2,1,0:T(8,128)S(1)} all-to-all(f32[8,2,32,512]{3,2,1,0:T(8,128)S(1)} %broadcast_in_dim.14), channel_id=1, replica_groups=mesh['yh'=4,'yl'=2,'x'=4,'z'=8,'core'=2] {'yl','x'}, dimensions={0} | all-to-all | bytes 2097152 | tf_op jit(solution)/shard_map/all_to_all | solution.py:127
  128.9 4.4 %collective-permute-start.6 = (f32[8,2,32,512]{3,2,1,0:T(8,128)S(1)}, f32[8,2,32,512]{3,2,1,0:T(8,128)S(1)}, u32[]{:S(2)}, u32[]{:S(2)}) collective-permute-start(f32[8,2,32,512]{3,2,1,0:T(8,128)S(1)} %all_to_all.27.mine), channel_id=1, source_target_pairs={{0,1},{1,0},{2,3},{3,2},{4,5},{5,4},{6,7},{7,6},{8,9},{9,8},{10,11... | collective-permute-start | bytes 3145736 | tf_op jit(solution)/shard_map/ppermute | solution.py:128
  133.3 2.3 %collective-permute-done.6.theirs = f32[8,2,32,512]{3,2,1,0:T(8,128)S(1)} collective-permute-done((f32[8,2,32,512]{3,2,1,0:T(8,128)S(1)}, f32[8,2,32,512]{3,2,1,0:T(8,128)S(1)}, u32[]{:S(2)}, u32[]{:S(2)}) %collective-permute-start.6) | collective-permute-done | bytes 1048608 | tf_op jit(solution)/shard_map/ppermute | solution.py:128
  135.6 1.3 shard_map.30
  136.8 1.9 collective-permute-start.7
  138.8 10.3 %collective-permute-done.7 = f32[2,32,512]{2,1,0:T(8,128)S(1)} collective-permute-done((f32[2,32,512]{2,1,0:T(8,128)S(1)}, f32[2,32,512]{2,1,0:T(8,128)S(1)}, u32[]{:S(2)}, u32[]{:S(2)}) %collective-permute-start.7) | collective-permute-done | bytes 131104 | tf_op jit(solution)/shard_map/ppermute | solution.py:34
  149.2 16.7 %all_to_all.28.mine = f32[8,2,32,512]{3,2,1,0:T(8,128)S(1)} all-to-all(f32[8,2,32,512]{3,2,1,0:T(8,128)S(1)} %broadcast_in_dim.15), channel_id=1, replica_groups=mesh['yh'=4,'yl'=2,'x'=4,'z'=8,'core'=2] {'yl','x'}, dimensions={0} | all-to-all | bytes 2097152 | tf_op jit(solution)/shard_map/all_to_all | solution.py:127
  165.9 4.2 %collective-permute-start.8 = (f32[8,2,32,512]{3,2,1,0:T(8,128)S(1)}, f32[8,2,32,512]{3,2,1,0:T(8,128)S(1)}, u32[]{:S(2)}, u32[]{:S(2)}) collective-permute-start(f32[8,2,32,512]{3,2,1,0:T(8,128)S(1)} %all_to_all.28.mine), channel_id=1, source_target_pairs={{0,1},{1,0},{2,3},{3,2},{4,5},{5,4},{6,7},{7,6},{8,9},{9,8},{10,11... | collective-permute-start | bytes 3145736 | tf_op jit(solution)/shard_map/ppermute | solution.py:128
  170.1 2.3 %collective-permute-done.8.theirs = f32[8,2,32,512]{3,2,1,0:T(8,128)S(1)} collective-permute-done((f32[8,2,32,512]{3,2,1,0:T(8,128)S(1)}, f32[8,2,32,512]{3,2,1,0:T(8,128)S(1)}, u32[]{:S(2)}, u32[]{:S(2)}) %collective-permute-start.8) | collective-permute-done | bytes 1048608 | tf_op jit(solution)/shard_map/ppermute | solution.py:128
  172.4 1.3 shard_map.31
  173.7 5.3 %collective-permute-start.9 = (f32[2,32,512]{2,1,0:T(8,128)S(1)}, f32[2,32,512]{2,1,0:T(8,128)S(1)}, u32[]{:S(2)}, u32[]{:S(2)}) collective-permute-start(f32[2,32,512]{2,1,0:T(8,128)S(1)} %shard_map.31), channel_id=1, source_target_pairs={{0,256},{16,272},{32,288},{48,304},{64,320},{80,336},{96,352},{112... | collective-permute-start | bytes 393224 | tf_op jit(solution)/shard_map/ppermute | solution.py:34
  179.0 8.3 %collective-permute-done.9 = f32[2,32,512]{2,1,0:T(8,128)S(1)} collective-permute-done((f32[2,32,512]{2,1,0:T(8,128)S(1)}, f32[2,32,512]{2,1,0:T(8,128)S(1)}, u32[]{:S(2)}, u32[]{:S(2)}) %collective-permute-start.9) | collective-permute-done | bytes 131104 | tf_op jit(solution)/shard_map/ppermute | solution.py:34
  187.5 16.8 %all_to_all.29.mine = f32[8,2,32,512]{3,2,1,0:T(8,128)S(1)} all-to-all(f32[8,2,32,512]{3,2,1,0:T(8,128)S(1)} %broadcast_in_dim.16), channel_id=1, replica_groups=mesh['yh'=4,'yl'=2,'x'=4,'z'=8,'core'=2] {'yl','x'}, dimensions={0} | all-to-all | bytes 2097152 | tf_op jit(solution)/shard_map/all_to_all | solution.py:127
  204.2 4.3 %collective-permute-start.10 = (f32[8,2,32,512]{3,2,1,0:T(8,128)S(1)}, f32[8,2,32,512]{3,2,1,0:T(8,128)S(1)}, u32[]{:S(2)}, u32[]{:S(2)}) collective-permute-start(f32[8,2,32,512]{3,2,1,0:T(8,128)S(1)} %all_to_all.29.mine), channel_id=1, source_target_pairs={{0,1},{1,0},{2,3},{3,2},{4,5},{5,4},{6,7},{7,6},{8,9},{9,8},{10,11... | collective-permute-start | bytes 3145736 | tf_op jit(solution)/shard_map/ppermute | solution.py:128
  208.5 2.3 %collective-permute-done.10.theirs = f32[8,2,32,512]{3,2,1,0:T(8,128)S(1)} collective-permute-done((f32[8,2,32,512]{3,2,1,0:T(8,128)S(1)}, f32[8,2,32,512]{3,2,1,0:T(8,128)S(1)}, u32[]{:S(2)}, u32[]{:S(2)}) %collective-permute-start.10) | collective-permute-done | bytes 1048608 | tf_op jit(solution)/shard_map/ppermute | solution.py:128
  212.0 1.9 collective-permute-start.11
  213.9 8.8 %collective-permute-done.11 = f32[32,512]{1,0:T(8,128)S(1)} collective-permute-done((f32[32,512]{1,0:T(8,128)S(1)}, f32[32,512]{1,0:T(8,128)S(1)}, u32[]{:S(2)}, u32[]{:S(2)}) %collective-permute-start.11) | collective-permute-done | bytes 65568 | tf_op jit(solution)/shard_map/ppermute | solution.py:34
  (29 shorter events, 4.9 us)
Async XLA Ops:
  0.0 0.9 copy-start
  0.9 15.3 %collective-permute-start.1 = (f32[2,32,512]{2,1,0:T(8,128)S(1)}, f32[2,32,512]{2,1,0:T(8,128)S(1)}, u32[]{:S(2)}, u32[]{:S(2)}) collective-permute-start(f32[2,32,512]{2,1,0:T(8,128)S(1)} %constant_dynamic-update-slice_fusion), channel_id=1, source_target_pairs={{0,0},{1,16},{2,32},{3,48},{4,64},{5,80},{6,96},{7,112},{8,1},{9,1... | collective-permute-start | bytes 393224 | tf_op jit(solution)/shard_map/ppermute | solution.py:34
  5.4 24.1 %collective-permute-start = (f32[2,32,512]{2,1,0:T(8,128)S(1)}, f32[2,32,512]{2,1,0:T(8,128)S(1)}, u32[]{:S(2)}, u32[]{:S(2)}) collective-permute-start(f32[2,32,512]{2,1,0:T(8,128)S(1)} %constant_dynamic-update-slice_fusion), channel_id=1, source_target_pairs={{0,2},{1,18},{2,34},{3,50},{4,66},{5,82},{6,98},{7,114},{8,3},{9,1... | collective-permute-start | bytes 393224 | tf_op jit(solution)/shard_map/ppermute | solution.py:34
  46.7 7.2 %collective-permute-start.2 = (f32[8,2,32,512]{3,2,1,0:T(8,128)S(1)}, f32[8,2,32,512]{3,2,1,0:T(8,128)S(1)}, u32[]{:S(2)}, u32[]{:S(2)}) collective-permute-start(f32[8,2,32,512]{3,2,1,0:T(8,128)S(1)} %all_to_all.25.mine), channel_id=1, source_target_pairs={{0,1},{1,0},{2,3},{3,2},{4,5},{5,4},{6,7},{7,6},{8,9},{9,8},{10,11... | collective-permute-start | bytes 3145736 | tf_op jit(solution)/shard_map/ppermute | solution.py:128
  55.2 14.0 %collective-permute-start.3 = (f32[2,32,512]{2,1,0:T(8,128)S(1)}, f32[2,32,512]{2,1,0:T(8,128)S(1)}, u32[]{:S(2)}, u32[]{:S(2)}) collective-permute-start(f32[2,32,512]{2,1,0:T(8,128)S(1)} %shard_map.28), channel_id=1, source_target_pairs={{0,4},{16,20},{32,36},{48,52},{64,68},{80,84},{96,100},{112,116},{... | collective-permute-start | bytes 393224 | tf_op jit(solution)/shard_map/ppermute | solution.py:34
  87.9 7.0 %collective-permute-start.4 = (f32[8,2,32,512]{3,2,1,0:T(8,128)S(1)}, f32[8,2,32,512]{3,2,1,0:T(8,128)S(1)}, u32[]{:S(2)}, u32[]{:S(2)}) collective-permute-start(f32[8,2,32,512]{3,2,1,0:T(8,128)S(1)} %all_to_all.26.mine), channel_id=1, source_target_pairs={{0,1},{1,0},{2,3},{3,2},{4,5},{5,4},{6,7},{7,6},{8,9},{9,8},{10,11... | collective-permute-start | bytes 3145736 | tf_op jit(solution)/shard_map/ppermute | solution.py:128
  96.2 13.6 %collective-permute-start.5 = (f32[2,32,512]{2,1,0:T(8,128)S(1)}, f32[2,32,512]{2,1,0:T(8,128)S(1)}, u32[]{:S(2)}, u32[]{:S(2)}) collective-permute-start(f32[2,32,512]{2,1,0:T(8,128)S(1)} %shard_map.29), channel_id=1, source_target_pairs={{0,8},{16,24},{32,40},{48,56},{64,72},{80,88},{96,104},{112,120},{... | collective-permute-start | bytes 393224 | tf_op jit(solution)/shard_map/ppermute | solution.py:34
  128.9 6.7 %collective-permute-start.6 = (f32[8,2,32,512]{3,2,1,0:T(8,128)S(1)}, f32[8,2,32,512]{3,2,1,0:T(8,128)S(1)}, u32[]{:S(2)}, u32[]{:S(2)}) collective-permute-start(f32[8,2,32,512]{3,2,1,0:T(8,128)S(1)} %all_to_all.27.mine), channel_id=1, source_target_pairs={{0,1},{1,0},{2,3},{3,2},{4,5},{5,4},{6,7},{7,6},{8,9},{9,8},{10,11... | collective-permute-start | bytes 3145736 | tf_op jit(solution)/shard_map/ppermute | solution.py:128
  136.8 12.2 %collective-permute-start.7 = (f32[2,32,512]{2,1,0:T(8,128)S(1)}, f32[2,32,512]{2,1,0:T(8,128)S(1)}, u32[]{:S(2)}, u32[]{:S(2)}) collective-permute-start(f32[2,32,512]{2,1,0:T(8,128)S(1)} %shard_map.30), channel_id=1, source_target_pairs={{0,128},{16,144},{32,160},{48,176},{64,192},{80,208},{96,224},{112... | collective-permute-start | bytes 393224 | tf_op jit(solution)/shard_map/ppermute | solution.py:34
  165.9 6.5 %collective-permute-start.8 = (f32[8,2,32,512]{3,2,1,0:T(8,128)S(1)}, f32[8,2,32,512]{3,2,1,0:T(8,128)S(1)}, u32[]{:S(2)}, u32[]{:S(2)}) collective-permute-start(f32[8,2,32,512]{3,2,1,0:T(8,128)S(1)} %all_to_all.28.mine), channel_id=1, source_target_pairs={{0,1},{1,0},{2,3},{3,2},{4,5},{5,4},{6,7},{7,6},{8,9},{9,8},{10,11... | collective-permute-start | bytes 3145736 | tf_op jit(solution)/shard_map/ppermute | solution.py:128
  173.7 13.6 %collective-permute-start.9 = (f32[2,32,512]{2,1,0:T(8,128)S(1)}, f32[2,32,512]{2,1,0:T(8,128)S(1)}, u32[]{:S(2)}, u32[]{:S(2)}) collective-permute-start(f32[2,32,512]{2,1,0:T(8,128)S(1)} %shard_map.31), channel_id=1, source_target_pairs={{0,256},{16,272},{32,288},{48,304},{64,320},{80,336},{96,352},{112... | collective-permute-start | bytes 393224 | tf_op jit(solution)/shard_map/ppermute | solution.py:34
  204.2 6.5 %collective-permute-start.10 = (f32[8,2,32,512]{3,2,1,0:T(8,128)S(1)}, f32[8,2,32,512]{3,2,1,0:T(8,128)S(1)}, u32[]{:S(2)}, u32[]{:S(2)}) collective-permute-start(f32[8,2,32,512]{3,2,1,0:T(8,128)S(1)} %all_to_all.29.mine), channel_id=1, source_target_pairs={{0,1},{1,0},{2,3},{3,2},{4,5},{5,4},{6,7},{7,6},{8,9},{9,8},{10,11... | collective-permute-start | bytes 3145736 | tf_op jit(solution)/shard_map/ppermute | solution.py:128
  212.0 10.7 %collective-permute-start.11 = (f32[32,512]{1,0:T(8,128)S(1)}, f32[32,512]{1,0:T(8,128)S(1)}, u32[]{:S(2)}, u32[]{:S(2)}) collective-permute-start(f32[32,512]{1,0:T(8,128)S(1)} %shard_map.32), channel_id=1, source_target_pairs={{398,0},{414,1},{430,2},{446,3},{462,4},{478,5},{494,6},{510,7},{3... | collective-permute-start | bytes 196616 | tf_op jit(solution)/shard_map/ppermute | solution.py:34

commit v2 on v1

v2 whole, which is shorter than its diff:
```python
import functools

import jax
import jax.numpy as jnp
import numpy as np
from jax import lax
from jax.experimental import pallas as pl
from jax.experimental.pallas import tpu as pltpu
from jax.sharding import Mesh, PartitionSpec as P

AXES = ("yh", "yl", "x", "zh", "zl", "core")
SIZES = (4, 2, 4, 4, 2, 2)
GROUP = ("yl", "x")
BLOCKS = 32
LEVELS = 5


def site(block):
    bit = [(block >> i) & 1 for i in range(5)]
    return 2 * bit[0] + bit[3], 2 * bit[2] + bit[1], bit[4]


def origin(block, rows):
    return (block % BLOCKS) * 16 + rows


def place(block, rows):
    yh, zh, zl = site(block % BLOCKS)
    core, chip = divmod(rows, 8)
    return int(np.ravel_multi_index((yh, chip // 4, chip % 4, zh, zl, core), SIZES))


def move(array, source, target):
    pairs = [(source(t, r), target(t, r)) for t in range(BLOCKS) for r in range(16)]
    return lax.ppermute(array, AXES, pairs)


def split(x):
    high = x.astype(jnp.bfloat16)
    return high, (x - high.astype(jnp.float32)).astype(jnp.bfloat16)


def product(left, right):
    high, low = left
    rows = high.shape[0]
    dot = functools.partial(jnp.dot, preferred_element_type=jnp.float32)
    both = dot(jnp.concatenate([high, low], 0), right[0])
    return both[:rows] + both[rows:] + dot(high, right[1])


def combine_kernel(last, info, mine, theirs, term, *refs):
    core, column, map_slot, term_slot, counts = (info[i] for i in range(5))
    turned = refs[-1]

    def times(left, slot):
        pieces = [
            product(split(left[:, 256 * i : 256 * i + 256]), split(half[:, slot].reshape(256, 512)))
            for i, half in enumerate((mine, theirs))
        ]
        return pieces[0] + pieces[1]

    def ordered(rows):
        return jnp.where(core == 0, rows, jnp.concatenate([rows[:, 256:], rows[:, :256]], 1))

    slab = pl.ds(pl.multiple_of((column // 4) * 128, 128), 128)
    for i, half in enumerate((mine, theirs)):
        turned[:, 256 * i : 256 * i + 256] = half[:, map_slot, :, slab].reshape(256, 128).T
    left = turned[pl.ds(pl.multiple_of((column % 4) * 32, 32), 32), :]
    weighted = times(left, term_slot)
    if last:
        out = refs[0]
        total = times(ordered(weighted), map_slot)
        out[...] = term[...] + jnp.where(counts != 0, total, 0.0)
    else:
        later_map, out = refs[0], refs[1]
        both = times(ordered(jnp.concatenate([weighted, later_map[...]], 0)), map_slot)
        out[0] = both[32:]
        out[1] = term[...] + jnp.where(counts != 0, both[:32], 0.0)


def combine(last, info, *arrays):
    vmem = pl.BlockSpec(memory_space=pltpu.VMEM)
    shape = (32, 512) if last else (2, 32, 512)
    return pl.pallas_call(
        functools.partial(combine_kernel, last),
        out_shape=jax.ShapeDtypeStruct(shape, jnp.float32),
        in_specs=[pl.BlockSpec(memory_space=pltpu.SMEM)] + [vmem] * len(arrays),
        out_specs=vmem,
        scratch_shapes=[pltpu.VMEM((128, 512), jnp.float32)],
        compiler_params=pltpu.CompilerParams(vmem_limit_bytes=32 * 1024 * 1024),
    )(jnp.stack(info).astype(jnp.int32), *arrays)


def local(local_term, coupling):
    core, yh, zh, zl = (lax.axis_index(a) for a in ("core", "yh", "zh", "zl"))
    column = core * 8 + lax.axis_index(GROUP)
    end = yh // 2 + 2 * (zh % 2) + 4 * (zh // 2) + 8 * (yh % 2) + 16 * zl
    both = jnp.concatenate([coupling, local_term], 0)
    for level in range(LEVELS - 1):
        length = 1 << level
        if level == 0:
            earlier = move(both, origin, lambda t, r: place(t + 1, r))
            own = move(both, origin, place)
        else:
            own = both
            earlier = move(both, place, lambda t, r: place(t + length, r))
        rows = jnp.stack([earlier[0], own[1]])
        mine = lax.all_to_all(jnp.broadcast_to(rows[None], (8, 2, 32, 512)), GROUP, 0, 0, tiled=True)
        theirs = lax.ppermute(mine, "core", [(0, 1), (1, 0)])
        counts = (end - 2 * length + 1) % BLOCKS + length < BLOCKS
        both = combine(False, [core, column, 0, 1, counts], mine, theirs, earlier[1], own[0])

    is_earlier = (end - 15) % BLOCKS < 16
    rows = jnp.where(is_earlier, both[0], both[1])
    mine = lax.all_to_all(jnp.broadcast_to(rows[None], (16, 32, 512)), GROUP + ("zl",), 0, 0, tiled=True)
    mine = mine.reshape(8, 2, 32, 512)
    theirs = lax.ppermute(mine, "core", [(0, 1), (1, 0)])
    map_slot = jnp.where(is_earlier, zl, 1 - zl)
    term = combine(True, [core, column, map_slot, 1 - map_slot, is_earlier], mine, theirs, both[1])
    return move(term, lambda t, r: place(t + 15, r), origin)[None]


def solution(mesh):
    fine = Mesh(mesh.devices.reshape(SIZES), AXES)
    spec = P(("yh", "yl", "x"), ("zh", "zl", "core"), None)
    return jax.shard_map(local, mesh=fine, in_specs=(spec, spec), out_specs=spec, check_vma=False)
```

time: 225 us -> 215 us (0.956)
  waiting for transfers between devices: 80.9 us -> 70.6 us
    ppermute x7 -> x6, waiting for transfers between devices: 69.9 us -> 59.9 us  [move(): return lax.ppermute(array, AXES, pairs)]
    ppermute x7 -> x6, starting transfers between devices: 22.7 us -> 26.3 us  [move(): return lax.ppermute(array, AXES, pairs)]
  transfers between devices with their start and end apart: 12 -> 11, of which waited for: 12 -> 11; matrix products, arithmetic and copies ran while one was open for 0% -> 0% of each run, Pallas kernels for 0% -> 0%
where the time goes in v2:
time: 215 us; the launch traced here: 213 us
  blocking collectives  86.6 us (40%)
  waiting for transfers between devices  70.6 us (33%)
  starting transfers between devices  46.9 us (22%)
  Pallas kernels  6.21 us (3%)
  local copies, waits for them, and re-layouts  2.61 us (1%)
    all_to_all x4, blocking collectives, local(): lax.all_to_all(jnp.broadcast_to(rows[None], (8, 2, 32, 512)), GROUP, 0, 0...  67.6 us
    ppermute x6, waiting for transfers between devices, move(): return lax.ppermute(array, AXES, pairs)  59.9 us
    ppermute x6, starting transfers between devices, move(): return lax.ppermute(array, AXES, pairs)  26.3 us
    ppermute x5, starting transfers between devices, local(): theirs = lax.ppermute(mine, 'core', [(0, 1), (1, 0)])  20.6 us
    all_to_all x1, blocking collectives, local(): lax.all_to_all(jnp.broadcast_to(rows[None], (16, 32, 512)), GROUP + ('zl'...  19.1 us
    ppermute x5, waiting for transfers between devices, local(): theirs = lax.ppermute(mine, 'core', [(0, 1), (1, 0)])  10.8 us
    pallas_call x5, Pallas kernels, combine(): pl.pallas_call(functools.partial(combine_kernel, last), out_shape=jax.Sha...  6.21 us
  transfers between devices with their start and end apart: 11, of which 11 were waited for; matrix products, arithmetic and copies ran while one was open for 0% of the time, Pallas kernels for 0%

profile of v2, /device:TPU:1, one launch (start us, length us, event | category | flops | bytes accessed | tf_op | source)
XLA Modules:
  0.0 213.5 jit_solution(7800639974901293475)
XLA Ops:
  0.9 4.5 %collective-permute-start.1 = (f32[2,32,512]{2,1,0:T(8,128)S(1)}, f32[2,32,512]{2,1,0:T(8,128)S(1)}, u32[]{:S(2)}, u32[]{:S(2)}) collective-permute-start(f32[2,32,512]{2,1,0:T(8,128)S(1)} %constant_dynamic-update-slice_fusion), channel_id=1, source_target_pairs={{0,0},{1,16},{2,32},{3,48},{4,64},{5,80},{6,96},{7,112},{8,1},{9,1... | collective-permute-start | bytes 393224 | tf_op jit(solution)/shard_map/ppermute | solution.py:35
  5.4 9.5 %collective-permute-start = (f32[2,32,512]{2,1,0:T(8,128)S(1)}, f32[2,32,512]{2,1,0:T(8,128)S(1)}, u32[]{:S(2)}, u32[]{:S(2)}) collective-permute-start(f32[2,32,512]{2,1,0:T(8,128)S(1)} %constant_dynamic-update-slice_fusion), channel_id=1, source_target_pairs={{0,256},{1,272},{2,288},{3,304},{4,320},{5,336},{6,352},{7,368},{8... | collective-permute-start | bytes 393224 | tf_op jit(solution)/shard_map/ppermute | solution.py:35
  14.9 1.3 collective-permute-done.1
  16.2 18.5 %collective-permute-done = f32[2,32,512]{2,1,0:T(8,128)S(1)} collective-permute-done((f32[2,32,512]{2,1,0:T(8,128)S(1)}, f32[2,32,512]{2,1,0:T(8,128)S(1)}, u32[]{:S(2)}, u32[]{:S(2)}) %collective-permute-start) | collective-permute-done | bytes 131104 | tf_op jit(solution)/shard_map/ppermute | solution.py:35
  34.8 17.3 %all_to_all.25.mine = f32[8,2,32,512]{3,2,1,0:T(8,128)S(1)} all-to-all(f32[8,2,32,512]{3,2,1,0:T(8,128)S(1)} %broadcast_in_dim.14), channel_id=1, replica_groups=mesh['yh'=4,'yl'=2,'x'=4,'zh'=4,'zl'=2,'core'=2] {'yl','x'}, dimensions={0} | all-to-all | bytes 2097152 | tf_op jit(solution)/shard_map/all_to_all | solution.py:108
  52.2 4.3 %collective-permute-start.2 = (f32[8,2,32,512]{3,2,1,0:T(8,128)S(1)}, f32[8,2,32,512]{3,2,1,0:T(8,128)S(1)}, u32[]{:S(2)}, u32[]{:S(2)}) collective-permute-start(f32[8,2,32,512]{3,2,1,0:T(8,128)S(1)} %all_to_all.25.mine), channel_id=1, source_target_pairs={{0,1},{1,0},{2,3},{3,2},{4,5},{5,4},{6,7},{7,6},{8,9},{9,8},{10,11... | collective-permute-start | bytes 3145736 | tf_op jit(solution)/shard_map/ppermute | solution.py:109
  56.6 2.1 collective-permute-done.2.theirs
  58.7 1.2 shard_map.28
  60.0 1.9 collective-permute-start.3
  61.9 11.3 %collective-permute-done.3 = f32[2,32,512]{2,1,0:T(8,128)S(1)} collective-permute-done((f32[2,32,512]{2,1,0:T(8,128)S(1)}, f32[2,32,512]{2,1,0:T(8,128)S(1)}, u32[]{:S(2)}, u32[]{:S(2)}) %collective-permute-start.3) | collective-permute-done | bytes 131104 | tf_op jit(solution)/shard_map/ppermute | solution.py:35
  73.4 16.8 %all_to_all.26.mine = f32[8,2,32,512]{3,2,1,0:T(8,128)S(1)} all-to-all(f32[8,2,32,512]{3,2,1,0:T(8,128)S(1)} %broadcast_in_dim.15), channel_id=1, replica_groups=mesh['yh'=4,'yl'=2,'x'=4,'zh'=4,'zl'=2,'core'=2] {'yl','x'}, dimensions={0} | all-to-all | bytes 2097152 | tf_op jit(solution)/shard_map/all_to_all | solution.py:108
  90.2 4.3 %collective-permute-start.4 = (f32[8,2,32,512]{3,2,1,0:T(8,128)S(1)}, f32[8,2,32,512]{3,2,1,0:T(8,128)S(1)}, u32[]{:S(2)}, u32[]{:S(2)}) collective-permute-start(f32[8,2,32,512]{3,2,1,0:T(8,128)S(1)} %all_to_all.26.mine), channel_id=1, source_target_pairs={{0,1},{1,0},{2,3},{3,2},{4,5},{5,4},{6,7},{7,6},{8,9},{9,8},{10,11... | collective-permute-start | bytes 3145736 | tf_op jit(solution)/shard_map/ppermute | solution.py:109
  94.6 2.2 %collective-permute-done.4.theirs = f32[8,2,32,512]{3,2,1,0:T(8,128)S(1)} collective-permute-done((f32[8,2,32,512]{3,2,1,0:T(8,128)S(1)}, f32[8,2,32,512]{3,2,1,0:T(8,128)S(1)}, u32[]{:S(2)}, u32[]{:S(2)}) %collective-permute-start.4) | collective-permute-done | bytes 1048608 | tf_op jit(solution)/shard_map/ppermute | solution.py:109
  96.7 1.2 shard_map.29
  98.0 1.9 collective-permute-start.5
  99.9 12.9 %collective-permute-done.5 = f32[2,32,512]{2,1,0:T(8,128)S(1)} collective-permute-done((f32[2,32,512]{2,1,0:T(8,128)S(1)}, f32[2,32,512]{2,1,0:T(8,128)S(1)}, u32[]{:S(2)}, u32[]{:S(2)}) %collective-permute-start.5) | collective-permute-done | bytes 131104 | tf_op jit(solution)/shard_map/ppermute | solution.py:35
  113.0 16.7 %all_to_all.27.mine = f32[8,2,32,512]{3,2,1,0:T(8,128)S(1)} all-to-all(f32[8,2,32,512]{3,2,1,0:T(8,128)S(1)} %broadcast_in_dim.16), channel_id=1, replica_groups=mesh['yh'=4,'yl'=2,'x'=4,'zh'=4,'zl'=2,'core'=2] {'yl','x'}, dimensions={0} | all-to-all | bytes 2097152 | tf_op jit(solution)/shard_map/all_to_all | solution.py:108
  129.8 4.2 %collective-permute-start.6 = (f32[8,2,32,512]{3,2,1,0:T(8,128)S(1)}, f32[8,2,32,512]{3,2,1,0:T(8,128)S(1)}, u32[]{:S(2)}, u32[]{:S(2)}) collective-permute-start(f32[8,2,32,512]{3,2,1,0:T(8,128)S(1)} %all_to_all.27.mine), channel_id=1, source_target_pairs={{0,1},{1,0},{2,3},{3,2},{4,5},{5,4},{6,7},{7,6},{8,9},{9,8},{10,11... | collective-permute-start | bytes 3145736 | tf_op jit(solution)/shard_map/ppermute | solution.py:109
  134.1 2.2 %collective-permute-done.6.theirs = f32[8,2,32,512]{3,2,1,0:T(8,128)S(1)} collective-permute-done((f32[8,2,32,512]{3,2,1,0:T(8,128)S(1)}, f32[8,2,32,512]{3,2,1,0:T(8,128)S(1)}, u32[]{:S(2)}, u32[]{:S(2)}) %collective-permute-start.6) | collective-permute-done | bytes 1048608 | tf_op jit(solution)/shard_map/ppermute | solution.py:109
  136.2 1.2 shard_map.30
  137.5 2.8 %collective-permute-start.7 = (f32[2,32,512]{2,1,0:T(8,128)S(1)}, f32[2,32,512]{2,1,0:T(8,128)S(1)}, u32[]{:S(2)}, u32[]{:S(2)}) collective-permute-start(f32[2,32,512]{2,1,0:T(8,128)S(1)} %shard_map.30), channel_id=1, source_target_pairs={{0,128},{16,144},{32,160},{48,176},{64,192},{80,208},{96,224},{112... | collective-permute-start | bytes 393224 | tf_op jit(solution)/shard_map/ppermute | solution.py:35
  140.3 9.9 %collective-permute-done.7 = f32[2,32,512]{2,1,0:T(8,128)S(1)} collective-permute-done((f32[2,32,512]{2,1,0:T(8,128)S(1)}, f32[2,32,512]{2,1,0:T(8,128)S(1)}, u32[]{:S(2)}, u32[]{:S(2)}) %collective-permute-start.7) | collective-permute-done | bytes 131104 | tf_op jit(solution)/shard_map/ppermute | solution.py:35
  150.4 16.7 %all_to_all.28.mine = f32[8,2,32,512]{3,2,1,0:T(8,128)S(1)} all-to-all(f32[8,2,32,512]{3,2,1,0:T(8,128)S(1)} %broadcast_in_dim.17), channel_id=1, replica_groups=mesh['yh'=4,'yl'=2,'x'=4,'zh'=4,'zl'=2,'core'=2] {'yl','x'}, dimensions={0} | all-to-all | bytes 2097152 | tf_op jit(solution)/shard_map/all_to_all | solution.py:108
  167.1 4.2 %collective-permute-start.8 = (f32[8,2,32,512]{3,2,1,0:T(8,128)S(1)}, f32[8,2,32,512]{3,2,1,0:T(8,128)S(1)}, u32[]{:S(2)}, u32[]{:S(2)}) collective-permute-start(f32[8,2,32,512]{3,2,1,0:T(8,128)S(1)} %all_to_all.28.mine), channel_id=1, source_target_pairs={{0,1},{1,0},{2,3},{3,2},{4,5},{5,4},{6,7},{7,6},{8,9},{9,8},{10,11... | collective-permute-start | bytes 3145736 | tf_op jit(solution)/shard_map/ppermute | solution.py:109
  171.4 2.2 %collective-permute-done.8.theirs = f32[8,2,32,512]{3,2,1,0:T(8,128)S(1)} collective-permute-done((f32[8,2,32,512]{3,2,1,0:T(8,128)S(1)}, f32[8,2,32,512]{3,2,1,0:T(8,128)S(1)}, u32[]{:S(2)}, u32[]{:S(2)}) %collective-permute-start.8) | collective-permute-done | bytes 1048608 | tf_op jit(solution)/shard_map/ppermute | solution.py:109
  173.6 1.2 shard_map.31
  175.0 19.1 %all_to_all.29 = f32[16,32,512]{2,1,0:T(8,128)S(1)} all-to-all(f32[16,32,512]{2,1,0:T(8,128)S(1)} %broadcast_in_dim.19), channel_id=1, replica_groups=mesh['yh'=4,'yl'=2,'x'=4,'zh'=4,'zl'=2,'core'=2] {'yl','x','zl'}, dimensions={0} | all-to-all | bytes 2097152 | tf_op jit(solution)/shard_map/all_to_all | solution.py:115
  194.0 3.7 %collective-permute-start.9 = (f32[8,2,32,512]{3,2,1,0:T(8,128)S(1)}, f32[8,2,32,512]{3,2,1,0:T(8,128)S(1)}, u32[]{:S(2)}, u32[]{:S(2)}) collective-permute-start(f32[8,2,32,512]{3,2,1,0:T(8,128)S(1)} %bitcast.31), channel_id=1, source_target_pairs={{0,1},{1,0},{2,3},{3,2},{4,5},{5,4},{6,7},{7,6},{8,9},{9,8},{10,11... | collective-permute-start | bytes 3145736 | tf_op jit(solution)/shard_map/ppermute | solution.py:117
  197.9 2.2 %collective-permute-done.9.theirs = f32[8,2,32,512]{3,2,1,0:T(8,128)S(1)} collective-permute-done((f32[8,2,32,512]{3,2,1,0:T(8,128)S(1)}, f32[8,2,32,512]{3,2,1,0:T(8,128)S(1)}, u32[]{:S(2)}, u32[]{:S(2)}) %collective-permute-start.9) | collective-permute-done | bytes 1048608 | tf_op jit(solution)/shard_map/ppermute | solution.py:117
  200.0 1.2 shard_map.32
  201.3 5.6 %collective-permute-start.10 = (f32[32,512]{1,0:T(8,128)S(1)}, f32[32,512]{1,0:T(8,128)S(1)}, u32[]{:S(2)}, u32[]{:S(2)}) collective-permute-start(f32[32,512]{1,0:T(8,128)S(1)} %shard_map.32), channel_id=1, source_target_pairs={{396,0},{412,1},{428,2},{444,3},{460,4},{476,5},{492,6},{508,7},{3... | collective-permute-start | bytes 196616 | tf_op jit(solution)/shard_map/ppermute | solution.py:35
  206.9 6.0 %collective-permute-done.10 = f32[32,512]{1,0:T(8,128)S(1)} collective-permute-done((f32[32,512]{1,0:T(8,128)S(1)}, f32[32,512]{1,0:T(8,128)S(1)}, u32[]{:S(2)}, u32[]{:S(2)}) %collective-permute-start.10) | collective-permute-done | bytes 65568 | tf_op jit(solution)/shard_map/ppermute | solution.py:35
  (28 shorter events, 2.7 us)
Async XLA Ops:
  0.0 0.9 copy-start
  0.9 15.3 %collective-permute-start.1 = (f32[2,32,512]{2,1,0:T(8,128)S(1)}, f32[2,32,512]{2,1,0:T(8,128)S(1)}, u32[]{:S(2)}, u32[]{:S(2)}) collective-permute-start(f32[2,32,512]{2,1,0:T(8,128)S(1)} %constant_dynamic-update-slice_fusion), channel_id=1, source_target_pairs={{0,0},{1,16},{2,32},{3,48},{4,64},{5,80},{6,96},{7,112},{8,1},{9,1... | collective-permute-start | bytes 393224 | tf_op jit(solution)/shard_map/ppermute | solution.py:35
  5.4 29.3 %collective-permute-start = (f32[2,32,512]{2,1,0:T(8,128)S(1)}, f32[2,32,512]{2,1,0:T(8,128)S(1)}, u32[]{:S(2)}, u32[]{:S(2)}) collective-permute-start(f32[2,32,512]{2,1,0:T(8,128)S(1)} %constant_dynamic-update-slice_fusion), channel_id=1, source_target_pairs={{0,256},{1,272},{2,288},{3,304},{4,320},{5,336},{6,352},{7,368},{8... | collective-permute-start | bytes 393224 | tf_op jit(solution)/shard_map/ppermute | solution.py:35
  52.2 6.6 %collective-permute-start.2 = (f32[8,2,32,512]{3,2,1,0:T(8,128)S(1)}, f32[8,2,32,512]{3,2,1,0:T(8,128)S(1)}, u32[]{:S(2)}, u32[]{:S(2)}) collective-permute-start(f32[8,2,32,512]{3,2,1,0:T(8,128)S(1)} %all_to_all.25.mine), channel_id=1, source_target_pairs={{0,1},{1,0},{2,3},{3,2},{4,5},{5,4},{6,7},{7,6},{8,9},{9,8},{10,11... | collective-permute-start | bytes 3145736 | tf_op jit(solution)/shard_map/ppermute | solution.py:109
  60.0 13.2 %collective-permute-start.3 = (f32[2,32,512]{2,1,0:T(8,128)S(1)}, f32[2,32,512]{2,1,0:T(8,128)S(1)}, u32[]{:S(2)}, u32[]{:S(2)}) collective-permute-start(f32[2,32,512]{2,1,0:T(8,128)S(1)} %shard_map.28), channel_id=1, source_target_pairs={{0,4},{16,20},{32,36},{48,52},{64,68},{80,84},{96,100},{112,116},{... | collective-permute-start | bytes 393224 | tf_op jit(solution)/shard_map/ppermute | solution.py:35
  90.2 6.5 %collective-permute-start.4 = (f32[8,2,32,512]{3,2,1,0:T(8,128)S(1)}, f32[8,2,32,512]{3,2,1,0:T(8,128)S(1)}, u32[]{:S(2)}, u32[]{:S(2)}) collective-permute-start(f32[8,2,32,512]{3,2,1,0:T(8,128)S(1)} %all_to_all.26.mine), channel_id=1, source_target_pairs={{0,1},{1,0},{2,3},{3,2},{4,5},{5,4},{6,7},{7,6},{8,9},{9,8},{10,11... | collective-permute-start | bytes 3145736 | tf_op jit(solution)/shard_map/ppermute | solution.py:109
  98.0 14.9 %collective-permute-start.5 = (f32[2,32,512]{2,1,0:T(8,128)S(1)}, f32[2,32,512]{2,1,0:T(8,128)S(1)}, u32[]{:S(2)}, u32[]{:S(2)}) collective-permute-start(f32[2,32,512]{2,1,0:T(8,128)S(1)} %shard_map.29), channel_id=1, source_target_pairs={{0,8},{16,24},{32,40},{48,56},{64,72},{80,88},{96,104},{112,120},{... | collective-permute-start | bytes 393224 | tf_op jit(solution)/shard_map/ppermute | solution.py:35
  129.8 6.5 %collective-permute-start.6 = (f32[8,2,32,512]{3,2,1,0:T(8,128)S(1)}, f32[8,2,32,512]{3,2,1,0:T(8,128)S(1)}, u32[]{:S(2)}, u32[]{:S(2)}) collective-permute-start(f32[8,2,32,512]{3,2,1,0:T(8,128)S(1)} %all_to_all.27.mine), channel_id=1, source_target_pairs={{0,1},{1,0},{2,3},{3,2},{4,5},{5,4},{6,7},{7,6},{8,9},{9,8},{10,11... | collective-permute-start | bytes 3145736 | tf_op jit(solution)/shard_map/ppermute | solution.py:109
  137.5 12.8 %collective-permute-start.7 = (f32[2,32,512]{2,1,0:T(8,128)S(1)}, f32[2,32,512]{2,1,0:T(8,128)S(1)}, u32[]{:S(2)}, u32[]{:S(2)}) collective-permute-start(f32[2,32,512]{2,1,0:T(8,128)S(1)} %shard_map.30), channel_id=1, source_target_pairs={{0,128},{16,144},{32,160},{48,176},{64,192},{80,208},{96,224},{112... | collective-permute-start | bytes 393224 | tf_op jit(solution)/shard_map/ppermute | solution.py:35
  167.1 6.5 %collective-permute-start.8 = (f32[8,2,32,512]{3,2,1,0:T(8,128)S(1)}, f32[8,2,32,512]{3,2,1,0:T(8,128)S(1)}, u32[]{:S(2)}, u32[]{:S(2)}) collective-permute-start(f32[8,2,32,512]{3,2,1,0:T(8,128)S(1)} %all_to_all.28.mine), channel_id=1, source_target_pairs={{0,1},{1,0},{2,3},{3,2},{4,5},{5,4},{6,7},{7,6},{8,9},{9,8},{10,11... | collective-permute-start | bytes 3145736 | tf_op jit(solution)/shard_map/ppermute | solution.py:109
  194.0 6.0 %collective-permute-start.9 = (f32[8,2,32,512]{3,2,1,0:T(8,128)S(1)}, f32[8,2,32,512]{3,2,1,0:T(8,128)S(1)}, u32[]{:S(2)}, u32[]{:S(2)}) collective-permute-start(f32[8,2,32,512]{3,2,1,0:T(8,128)S(1)} %bitcast.31), channel_id=1, source_target_pairs={{0,1},{1,0},{2,3},{3,2},{4,5},{5,4},{6,7},{7,6},{8,9},{9,8},{10,11... | collective-permute-start | bytes 3145736 | tf_op jit(solution)/shard_map/ppermute | solution.py:117
  201.3 11.6 %collective-permute-start.10 = (f32[32,512]{1,0:T(8,128)S(1)}, f32[32,512]{1,0:T(8,128)S(1)}, u32[]{:S(2)}, u32[]{:S(2)}) collective-permute-start(f32[32,512]{1,0:T(8,128)S(1)} %shard_map.32), channel_id=1, source_target_pairs={{396,0},{412,1},{428,2},{444,3},{460,4},{476,5},{492,6},{508,7},{3... | collective-permute-start | bytes 196616 | tf_op jit(solution)/shard_map/ppermute | solution.py:35

commit v3 on v2

v3 whole, which is shorter than its diff:
```python
import functools

import jax
import jax.numpy as jnp
import numpy as np
from jax import lax
from jax.experimental import pallas as pl
from jax.experimental.pallas import tpu as pltpu
from jax.sharding import Mesh, PartitionSpec as P

AXES = ("yh", "yl", "xh", "xl", "zh", "zl", "core")
SIZES = (4, 2, 2, 2, 4, 2, 2)
GROUP = ("yl", "xl", "xh")
BLOCKS = 32
LEVELS = 5


def site(block):
    bit = [(block >> i) & 1 for i in range(5)]
    return 2 * bit[2] + bit[1], 2 * bit[0] + bit[3], bit[4]


def origin(block, rows):
    return (block % BLOCKS) * 16 + rows


def place(block, rows):
    yh, zh, zl = site(block % BLOCKS)
    core, chip = divmod(rows, 8)
    return int(np.ravel_multi_index((yh, chip // 4, chip % 2, chip // 2 % 2, zh, zl, core), SIZES))


def move(array, source, target):
    pairs = [(source(t, r), target(t, r)) for t in range(BLOCKS) for r in range(16)]
    return lax.ppermute(array, AXES, pairs)


def split(x):
    high = x.astype(jnp.bfloat16)
    return high, (x - high.astype(jnp.float32)).astype(jnp.bfloat16)


def product(left, right, transposed=False):
    high, low = left
    rows = high.shape[0]
    dims = (((1,), (1 if transposed else 0,)), ((), ()))
    dot = functools.partial(lax.dot_general, dimension_numbers=dims, preferred_element_type=jnp.float32)
    both = dot(jnp.concatenate([high, low], 0), right[0])
    return both[:rows] + both[rows:] + dot(high, right[1])


def blocks(halves, at, width):
    found = []
    for half in halves:
        high, low = split(half[:, :, at : at + width].reshape(256, width))
        found += [(high[:128], low[:128]), (high[128:], low[128:])]
    return found


def rows_of_map(column, halves, turned):
    slab = pl.ds(pl.multiple_of((column // 4) * 128, 128), 128)
    for i, half in enumerate(halves):
        turned[:, 256 * i : 256 * i + 256] = half(slab).reshape(256, 128).T
    return turned[pl.ds(pl.multiple_of((column % 4) * 32, 32), 32), :]


def own_first(core, rows):
    return jnp.where(core == 0, rows, jnp.concatenate([rows[:, 256:], rows[:, :256]], 1))


def times(left, halves):
    pieces = [
        product(split(left[:, 256 * i : 256 * i + 256]), split(half.reshape(256, 512))) for i, half in enumerate(halves)
    ]
    return pieces[0] + pieces[1]


def level_kernel(info, mine, theirs, term, later_map, out, sent, turned, twice):
    core, column, counts = info[0], info[1], info[2]
    halves = (mine, theirs)
    left = rows_of_map(column, [lambda at, half=half: half[:, :, at] for half in halves], turned)
    lefts = [split(left[:, 128 * i : 128 * i + 128]) for i in range(4)]
    stored = blocks(halves, 512, 384)
    weighted = [0.0] * 4
    for i in range(4):
        row = product(lefts[i], stored[i])
        for j in range(3):
            weighted[(i + j) % 4] += row[:, 128 * j : 128 * j + 128]
        above = tuple(part[:, 128:256] for part in stored[i])
        weighted[i] += product(lefts[(i + 1) % 4], above, True)
    left = jnp.concatenate([jnp.concatenate(weighted, 1), own_first(core, later_map[...])], 0)
    both = times(left, [half[:, :, :512] for half in halves])
    total = term[...] + jnp.where(counts != 0, both[:32], 0.0)
    out[0] = both[32:]
    out[1] = total
    twice[:, :512] = total
    twice[:, 512:] = total
    sent[...] = twice[:, pl.ds(pl.multiple_of((column // 4) * 128, 128), 384)]


def last_kernel(info, mine, theirs, term, out, turned):
    core, column, map_slot, term_slot, counts = (info[i] for i in range(5))
    halves = (mine, theirs)
    left = rows_of_map(column, [lambda at, half=half: half[:, map_slot, :, at] for half in halves], turned)
    weighted = times(left, [half[:, term_slot] for half in halves])
    total = times(own_first(core, weighted), [half[:, map_slot] for half in halves])
    out[...] = term[...] + jnp.where(counts != 0, total, 0.0)


def call(kernel, shapes, widths, info, *arrays):
    vmem = pl.BlockSpec(memory_space=pltpu.VMEM)
    return pl.pallas_call(
        kernel,
        out_shape=[jax.ShapeDtypeStruct(shape, jnp.float32) for shape in shapes],
        in_specs=[pl.BlockSpec(memory_space=pltpu.SMEM)] + [vmem] * len(arrays),
        out_specs=[vmem] * len(shapes),
        scratch_shapes=[pltpu.VMEM(shape, jnp.float32) for shape in widths],
        compiler_params=pltpu.CompilerParams(vmem_limit_bytes=32 * 1024 * 1024),
    )(jnp.stack(info).astype(jnp.int32), *arrays)


def local(local_term, coupling):
    core, yh, zh, zl = (lax.axis_index(a) for a in ("core", "yh", "zh", "zl"))
    column = core * 8 + lax.axis_index(GROUP)
    end = zh // 2 + 2 * (yh % 2) + 4 * (yh // 2) + 8 * (zh % 2) + 16 * zl
    both = jnp.concatenate([coupling, local_term], 0)
    for level in range(LEVELS - 1):
        length = 1 << level
        if level == 0:
            earlier = move(both, origin, lambda t, r: place(t + 1, r))
            own = move(both, origin, place)
            sent = lax.dynamic_slice_in_dim(jnp.tile(own[1], (1, 2)), column // 4 * 128, 384, 1)
        else:
            own = both
            earlier = move(both, place, lambda t, r: place(t + length, r))
        rows = jnp.concatenate([earlier[0], sent], 1)
        mine = lax.all_to_all(jnp.broadcast_to(rows[None], (8, 32, 896)), GROUP, 0, 0, tiled=True)
        theirs = lax.ppermute(mine, "core", [(0, 1), (1, 0)])
        counts = (end - 2 * length + 1) % BLOCKS + length < BLOCKS
        both, sent = call(
            level_kernel,
            [(2, 32, 512), (32, 384)],
            [(128, 512), (32, 1024)],
            [core, column, counts],
            *(mine, theirs, earlier[1], own[0]),
        )

    is_earlier = (end - 15) % BLOCKS < 16
    rows = jnp.where(is_earlier, both[0], both[1])
    mine = lax.all_to_all(jnp.broadcast_to(rows[None], (16, 32, 512)), GROUP + ("zl",), 0, 0, tiled=True)
    mine = mine.reshape(8, 2, 32, 512)
    theirs = lax.ppermute(mine, "core", [(0, 1), (1, 0)])
    map_slot = jnp.where(is_earlier, zl, 1 - zl)
    info = [core, column, map_slot, 1 - map_slot, is_earlier]
    (term,) = call(last_kernel, [(32, 512)], [(128, 512)], info, mine, theirs, both[1])
    return move(term, lambda t, r: place(t + 15, r), origin)[None]


def solution(mesh):
    fine = Mesh(mesh.devices.reshape(SIZES), AXES)
    spec = P(("yh", "yl", "xh", "xl"), ("zh", "zl", "core"), None)
    return jax.shard_map(local, mesh=fine, in_specs=(spec, spec), out_specs=spec, check_vma=False)
```

time: 215 us -> 208 us (0.967)
  waiting for transfers between devices: 70.6 us -> 61 us
  starting transfers between devices: 46.9 us -> 50.3 us
    ppermute x6, waiting for transfers between devices: 59.9 us -> 50.9 us  [move(): return lax.ppermute(array, AXES, pairs)]
    ppermute x6, starting transfers between devices: 26.3 us -> 30.1 us  [move(): return lax.ppermute(array, AXES, pairs)]
  transfers between devices with their start and end apart: 11 -> 11, of which waited for: 11 -> 10; matrix products, arithmetic and copies ran while one was open for 0% -> 0% of each run, Pallas kernels for 0% -> 0%
where the time goes in v3:
time: 208 us
  blocking collectives  86.1 us (41%)
  waiting for transfers between devices  61 us (29%)
  starting transfers between devices  50.3 us (24%)
  Pallas kernels  7.37 us (4%)
  local copies, waits for them, and re-layouts  2.14 us (1%)
    all_to_all x4, blocking collectives, local(): lax.all_to_all(jnp.broadcast_to(rows[None], (8, 32, 896)), GROUP, 0, 0, t...  66.9 us
    ppermute x6, waiting for transfers between devices, move(): return lax.ppermute(array, AXES, pairs)  50.9 us
    ppermute x6, starting transfers between devices, move(): return lax.ppermute(array, AXES, pairs)  30.1 us
    ppermute x5, starting transfers between devices, local(): theirs = lax.ppermute(mine, 'core', [(0, 1), (1, 0)])  20.1 us
    all_to_all x1, blocking collectives, local(): lax.all_to_all(jnp.broadcast_to(rows[None], (16, 32, 512)), GROUP + ('zl'...  19.2 us
    ppermute x5, waiting for transfers between devices, local(): theirs = lax.ppermute(mine, 'core', [(0, 1), (1, 0)])  10.2 us
    pallas_call x5, Pallas kernels, call(): pl.pallas_call(kernel, out_shape=[jax.ShapeDtypeStruct(shape, jnp.float32...  7.37 us
  transfers between devices with their start and end apart: 11, of which 10 were waited for; matrix products, arithmetic and copies ran while one was open for 0% of the time, Pallas kernels for 0%

profile of v3, /device:TPU:1, one launch (start us, length us, event | category | flops | bytes accessed | tf_op | source)
XLA Modules:
  0.0 207.5 jit_solution(9936559647547316888)
XLA Ops:
  0.0 0.9 constant_dynamic-update-slice_fusion.1
  0.9 6.0 %collective-permute-start.1 = (f32[2,32,512]{2,1,0:T(8,128)S(1)}, f32[2,32,512]{2,1,0:T(8,128)S(1)}, u32[]{:S(2)}, u32[]{:S(2)}) collective-permute-start(f32[2,32,512]{2,1,0:T(8,128)S(1)} %constant_dynamic-update-slice_fusion), channel_id=1, source_target_pairs={{0,0},{1,32},{2,16},{3,48},{4,64},{5,96},{6,80},{7,112},{8,1},{9,3... | collective-permute-start | bytes 393224 | tf_op jit(solution)/shard_map/ppermute | solution.py:35
  6.9 10.4 %collective-permute-start = (f32[2,32,512]{2,1,0:T(8,128)S(1)}, f32[2,32,512]{2,1,0:T(8,128)S(1)}, u32[]{:S(2)}, u32[]{:S(2)}) collective-permute-start(f32[2,32,512]{2,1,0:T(8,128)S(1)} %constant_dynamic-update-slice_fusion), channel_id=1, source_target_pairs={{0,8},{1,40},{2,24},{3,56},{4,72},{5,104},{6,88},{7,120},{8,9},{9,... | collective-permute-start | bytes 393224 | tf_op jit(solution)/shard_map/ppermute | solution.py:35
  17.5 16.7 %collective-permute-done = f32[2,32,512]{2,1,0:T(8,128)S(1)} collective-permute-done((f32[2,32,512]{2,1,0:T(8,128)S(1)}, f32[2,32,512]{2,1,0:T(8,128)S(1)}, u32[]{:S(2)}, u32[]{:S(2)}) %collective-permute-start) | collective-permute-done | bytes 131104 | tf_op jit(solution)/shard_map/ppermute | solution.py:35
  34.3 17.9 %all_to_all.25.mine = f32[8,32,896]{2,1,0:T(8,128)S(1)} all-to-all(f32[8,32,896]{2,1,0:T(8,128)S(1)} %broadcast_in_dim.14), channel_id=1, replica_groups=mesh['yh'=4,'yl'=2,'xh'=2,'xl'=2,'zh'=4,'zl'=2,'core'=2] {'yl','xl','xh'}, dimensions={0} | all-to-all | bytes 1835008 | tf_op jit(solution)/shard_map/all_to_all | solution.py:137
  52.2 2.4 %collective-permute-start.2 = (f32[8,32,896]{2,1,0:T(8,128)S(1)}, f32[8,32,896]{2,1,0:T(8,128)S(1)}, u32[]{:S(2)}, u32[]{:S(2)}) collective-permute-start(f32[8,32,896]{2,1,0:T(8,128)S(1)} %all_to_all.25.mine), channel_id=1, source_target_pairs={{0,1},{1,0},{2,3},{3,2},{4,5},{5,4},{6,7},{7,6},{8,9},{9,8},{10,11... | collective-permute-start | bytes 2752520 | tf_op jit(solution)/shard_map/ppermute | solution.py:138
  54.8 1.9 collective-permute-done.2.theirs
  56.7 1.4 shard_map.28
  58.1 3.7 %collective-permute-start.3 = (f32[2,32,512]{2,1,0:T(8,128)S(1)}, f32[2,32,512]{2,1,0:T(8,128)S(1)}, u32[]{:S(2)}, u32[]{:S(2)}) collective-permute-start(f32[2,32,512]{2,1,0:T(8,128)S(1)} %get-tuple-element.12), channel_id=1, source_target_pairs={{0,128},{32,160},{16,144},{48,176},{64,192},{96,224},{80,208},{112... | collective-permute-start | bytes 393224 | tf_op jit(solution)/shard_map/ppermute | solution.py:35
  61.9 9.0 %collective-permute-done.3 = f32[2,32,512]{2,1,0:T(8,128)S(1)} collective-permute-done((f32[2,32,512]{2,1,0:T(8,128)S(1)}, f32[2,32,512]{2,1,0:T(8,128)S(1)}, u32[]{:S(2)}, u32[]{:S(2)}) %collective-permute-start.3) | collective-permute-done | bytes 131104 | tf_op jit(solution)/shard_map/ppermute | solution.py:35
  71.0 15.8 %all_to_all.26.mine = f32[8,32,896]{2,1,0:T(8,128)S(1)} all-to-all(f32[8,32,896]{2,1,0:T(8,128)S(1)} %broadcast_in_dim.15), channel_id=1, replica_groups=mesh['yh'=4,'yl'=2,'xh'=2,'xl'=2,'zh'=4,'zl'=2,'core'=2] {'yl','xl','xh'}, dimensions={0} | all-to-all | bytes 1835008 | tf_op jit(solution)/shard_map/all_to_all | solution.py:137
  86.8 5.2 %collective-permute-start.4 = (f32[8,32,896]{2,1,0:T(8,128)S(1)}, f32[8,32,896]{2,1,0:T(8,128)S(1)}, u32[]{:S(2)}, u32[]{:S(2)}) collective-permute-start(f32[8,32,896]{2,1,0:T(8,128)S(1)} %all_to_all.26.mine), channel_id=1, source_target_pairs={{0,1},{1,0},{2,3},{3,2},{4,5},{5,4},{6,7},{7,6},{8,9},{9,8},{10,11... | collective-permute-start | bytes 2752520 | tf_op jit(solution)/shard_map/ppermute | solution.py:138
  92.1 1.9 collective-permute-done.4.theirs
  94.1 1.4 shard_map.29
  95.4 3.4 %collective-permute-start.5 = (f32[2,32,512]{2,1,0:T(8,128)S(1)}, f32[2,32,512]{2,1,0:T(8,128)S(1)}, u32[]{:S(2)}, u32[]{:S(2)}) collective-permute-start(f32[2,32,512]{2,1,0:T(8,128)S(1)} %get-tuple-element.14), channel_id=1, source_target_pairs={{0,256},{32,288},{16,272},{48,304},{64,320},{96,352},{80,336},{112... | collective-permute-start | bytes 393224 | tf_op jit(solution)/shard_map/ppermute | solution.py:35
  98.9 10.2 %collective-permute-done.5 = f32[2,32,512]{2,1,0:T(8,128)S(1)} collective-permute-done((f32[2,32,512]{2,1,0:T(8,128)S(1)}, f32[2,32,512]{2,1,0:T(8,128)S(1)}, u32[]{:S(2)}, u32[]{:S(2)}) %collective-permute-start.5) | collective-permute-done | bytes 131104 | tf_op jit(solution)/shard_map/ppermute | solution.py:35
  109.2 18.3 %all_to_all.27.mine = f32[8,32,896]{2,1,0:T(8,128)S(1)} all-to-all(f32[8,32,896]{2,1,0:T(8,128)S(1)} %broadcast_in_dim.16), channel_id=1, replica_groups=mesh['yh'=4,'yl'=2,'xh'=2,'xl'=2,'zh'=4,'zl'=2,'core'=2] {'yl','xl','xh'}, dimensions={0} | all-to-all | bytes 1835008 | tf_op jit(solution)/shard_map/all_to_all | solution.py:137
  127.5 4.2 %collective-permute-start.6 = (f32[8,32,896]{2,1,0:T(8,128)S(1)}, f32[8,32,896]{2,1,0:T(8,128)S(1)}, u32[]{:S(2)}, u32[]{:S(2)}) collective-permute-start(f32[8,32,896]{2,1,0:T(8,128)S(1)} %all_to_all.27.mine), channel_id=1, source_target_pairs={{0,1},{1,0},{2,3},{3,2},{4,5},{5,4},{6,7},{7,6},{8,9},{9,8},{10,11... | collective-permute-start | bytes 2752520 | tf_op jit(solution)/shard_map/ppermute | solution.py:138
  131.6 2.1 collective-permute-done.6.theirs
  133.7 1.4 shard_map.30
  135.1 3.8 %collective-permute-start.7 = (f32[2,32,512]{2,1,0:T(8,128)S(1)}, f32[2,32,512]{2,1,0:T(8,128)S(1)}, u32[]{:S(2)}, u32[]{:S(2)}) collective-permute-start(f32[2,32,512]{2,1,0:T(8,128)S(1)} %get-tuple-element.16), channel_id=1, source_target_pairs={{0,4},{32,36},{16,20},{48,52},{64,68},{96,100},{80,84},{112,116},{... | collective-permute-start | bytes 393224 | tf_op jit(solution)/shard_map/ppermute | solution.py:35
  138.9 4.6 %collective-permute-done.7 = f32[2,32,512]{2,1,0:T(8,128)S(1)} collective-permute-done((f32[2,32,512]{2,1,0:T(8,128)S(1)}, f32[2,32,512]{2,1,0:T(8,128)S(1)}, u32[]{:S(2)}, u32[]{:S(2)}) %collective-permute-start.7) | collective-permute-done | bytes 131104 | tf_op jit(solution)/shard_map/ppermute | solution.py:35
  143.7 14.8 %all_to_all.28.mine = f32[8,32,896]{2,1,0:T(8,128)S(1)} all-to-all(f32[8,32,896]{2,1,0:T(8,128)S(1)} %broadcast_in_dim.17), channel_id=1, replica_groups=mesh['yh'=4,'yl'=2,'xh'=2,'xl'=2,'zh'=4,'zl'=2,'core'=2] {'yl','xl','xh'}, dimensions={0} | all-to-all | bytes 1835008 | tf_op jit(solution)/shard_map/all_to_all | solution.py:137
  158.5 4.7 %collective-permute-start.8 = (f32[8,32,896]{2,1,0:T(8,128)S(1)}, f32[8,32,896]{2,1,0:T(8,128)S(1)}, u32[]{:S(2)}, u32[]{:S(2)}) collective-permute-start(f32[8,32,896]{2,1,0:T(8,128)S(1)} %all_to_all.28.mine), channel_id=1, source_target_pairs={{0,1},{1,0},{2,3},{3,2},{4,5},{5,4},{6,7},{7,6},{8,9},{9,8},{10,11... | collective-permute-start | bytes 2752520 | tf_op jit(solution)/shard_map/ppermute | solution.py:138
  163.2 2.1 collective-permute-done.8.theirs
  165.2 2.0 shard_map.31
  167.4 19.2 %all_to_all.29 = f32[16,32,512]{2,1,0:T(8,128)S(1)} all-to-all(f32[16,32,512]{2,1,0:T(8,128)S(1)} %broadcast_in_dim.19), channel_id=1, replica_groups=mesh['yh'=4,'yl'=2,'xh'=2,'xl'=2,'zh'=4,'zl'=2,'core'=2] {'yl','xl','xh'..., dimensions={0} | all-to-all | bytes 2097152 | tf_op jit(solution)/shard_map/all_to_all | solution.py:150
  186.6 3.7 %collective-permute-start.9 = (f32[8,2,32,512]{3,2,1,0:T(8,128)S(1)}, f32[8,2,32,512]{3,2,1,0:T(8,128)S(1)}, u32[]{:S(2)}, u32[]{:S(2)}) collective-permute-start(f32[8,2,32,512]{3,2,1,0:T(8,128)S(1)} %bitcast.43), channel_id=1, source_target_pairs={{0,1},{1,0},{2,3},{3,2},{4,5},{5,4},{6,7},{7,6},{8,9},{9,8},{10,11... | collective-permute-start | bytes 3145736 | tf_op jit(solution)/shard_map/ppermute | solution.py:152
  190.4 2.2 %collective-permute-done.9.theirs = f32[8,2,32,512]{3,2,1,0:T(8,128)S(1)} collective-permute-done((f32[8,2,32,512]{3,2,1,0:T(8,128)S(1)}, f32[8,2,32,512]{3,2,1,0:T(8,128)S(1)}, u32[]{:S(2)}, u32[]{:S(2)}) %collective-permute-start.9) | collective-permute-done | bytes 1048608 | tf_op jit(solution)/shard_map/ppermute | solution.py:152
  192.5 1.2 shard_map.32
  193.8 2.7 %collective-permute-start.10 = (f32[32,512]{1,0:T(8,128)S(1)}, f32[32,512]{1,0:T(8,128)S(1)}, u32[]{:S(2)}, u32[]{:S(2)}) collective-permute-start(f32[32,512]{1,0:T(8,128)S(1)} %shard_map.32), channel_id=1, source_target_pairs={{396,0},{428,1},{412,2},{444,3},{460,4},{492,5},{476,6},{508,7},{3... | collective-permute-start | bytes 196616 | tf_op jit(solution)/shard_map/ppermute | solution.py:35
  196.5 10.4 %collective-permute-done.10 = f32[32,512]{1,0:T(8,128)S(1)} collective-permute-done((f32[32,512]{1,0:T(8,128)S(1)}, f32[32,512]{1,0:T(8,128)S(1)}, u32[]{:S(2)}, u32[]{:S(2)}) %collective-permute-start.10) | collective-permute-done | bytes 65568 | tf_op jit(solution)/shard_map/ppermute | solution.py:35
  (29 shorter events, 1.5 us)
Async XLA Ops:
  0.0 0.9 copy-start
  0.9 16.5 %collective-permute-start.1 = (f32[2,32,512]{2,1,0:T(8,128)S(1)}, f32[2,32,512]{2,1,0:T(8,128)S(1)}, u32[]{:S(2)}, u32[]{:S(2)}) collective-permute-start(f32[2,32,512]{2,1,0:T(8,128)S(1)} %constant_dynamic-update-slice_fusion), channel_id=1, source_target_pairs={{0,0},{1,32},{2,16},{3,48},{4,64},{5,96},{6,80},{7,112},{8,1},{9,3... | collective-permute-start | bytes 393224 | tf_op jit(solution)/shard_map/ppermute | solution.py:35
  6.9 27.2 %collective-permute-start = (f32[2,32,512]{2,1,0:T(8,128)S(1)}, f32[2,32,512]{2,1,0:T(8,128)S(1)}, u32[]{:S(2)}, u32[]{:S(2)}) collective-permute-start(f32[2,32,512]{2,1,0:T(8,128)S(1)} %constant_dynamic-update-slice_fusion), channel_id=1, source_target_pairs={{0,8},{1,40},{2,24},{3,56},{4,72},{5,104},{6,88},{7,120},{8,9},{9,... | collective-permute-start | bytes 393224 | tf_op jit(solution)/shard_map/ppermute | solution.py:35
  52.2 4.5 %collective-permute-start.2 = (f32[8,32,896]{2,1,0:T(8,128)S(1)}, f32[8,32,896]{2,1,0:T(8,128)S(1)}, u32[]{:S(2)}, u32[]{:S(2)}) collective-permute-start(f32[8,32,896]{2,1,0:T(8,128)S(1)} %all_to_all.25.mine), channel_id=1, source_target_pairs={{0,1},{1,0},{2,3},{3,2},{4,5},{5,4},{6,7},{7,6},{8,9},{9,8},{10,11... | collective-permute-start | bytes 2752520 | tf_op jit(solution)/shard_map/ppermute | solution.py:138
  58.1 12.7 %collective-permute-start.3 = (f32[2,32,512]{2,1,0:T(8,128)S(1)}, f32[2,32,512]{2,1,0:T(8,128)S(1)}, u32[]{:S(2)}, u32[]{:S(2)}) collective-permute-start(f32[2,32,512]{2,1,0:T(8,128)S(1)} %get-tuple-element.12), channel_id=1, source_target_pairs={{0,128},{32,160},{16,144},{48,176},{64,192},{96,224},{80,208},{112... | collective-permute-start | bytes 393224 | tf_op jit(solution)/shard_map/ppermute | solution.py:35
  86.8 7.2 %collective-permute-start.4 = (f32[8,32,896]{2,1,0:T(8,128)S(1)}, f32[8,32,896]{2,1,0:T(8,128)S(1)}, u32[]{:S(2)}, u32[]{:S(2)}) collective-permute-start(f32[8,32,896]{2,1,0:T(8,128)S(1)} %all_to_all.26.mine), channel_id=1, source_target_pairs={{0,1},{1,0},{2,3},{3,2},{4,5},{5,4},{6,7},{7,6},{8,9},{9,8},{10,11... | collective-permute-start | bytes 2752520 | tf_op jit(solution)/shard_map/ppermute | solution.py:138
  95.4 13.6 %collective-permute-start.5 = (f32[2,32,512]{2,1,0:T(8,128)S(1)}, f32[2,32,512]{2,1,0:T(8,128)S(1)}, u32[]{:S(2)}, u32[]{:S(2)}) collective-permute-start(f32[2,32,512]{2,1,0:T(8,128)S(1)} %get-tuple-element.14), channel_id=1, source_target_pairs={{0,256},{32,288},{16,272},{48,304},{64,320},{96,352},{80,336},{112... | collective-permute-start | bytes 393224 | tf_op jit(solution)/shard_map/ppermute | solution.py:35
  127.5 6.2 %collective-permute-start.6 = (f32[8,32,896]{2,1,0:T(8,128)S(1)}, f32[8,32,896]{2,1,0:T(8,128)S(1)}, u32[]{:S(2)}, u32[]{:S(2)}) collective-permute-start(f32[8,32,896]{2,1,0:T(8,128)S(1)} %all_to_all.27.mine), channel_id=1, source_target_pairs={{0,1},{1,0},{2,3},{3,2},{4,5},{5,4},{6,7},{7,6},{8,9},{9,8},{10,11... | collective-permute-start | bytes 2752520 | tf_op jit(solution)/shard_map/ppermute | solution.py:138
  135.1 8.4 %collective-permute-start.7 = (f32[2,32,512]{2,1,0:T(8,128)S(1)}, f32[2,32,512]{2,1,0:T(8,128)S(1)}, u32[]{:S(2)}, u32[]{:S(2)}) collective-permute-start(f32[2,32,512]{2,1,0:T(8,128)S(1)} %get-tuple-element.16), channel_id=1, source_target_pairs={{0,4},{32,36},{16,20},{48,52},{64,68},{96,100},{80,84},{112,116},{... | collective-permute-start | bytes 393224 | tf_op jit(solution)/shard_map/ppermute | solution.py:35
  158.5 6.8 %collective-permute-start.8 = (f32[8,32,896]{2,1,0:T(8,128)S(1)}, f32[8,32,896]{2,1,0:T(8,128)S(1)}, u32[]{:S(2)}, u32[]{:S(2)}) collective-permute-start(f32[8,32,896]{2,1,0:T(8,128)S(1)} %all_to_all.28.mine), channel_id=1, source_target_pairs={{0,1},{1,0},{2,3},{3,2},{4,5},{5,4},{6,7},{7,6},{8,9},{9,8},{10,11... | collective-permute-start | bytes 2752520 | tf_op jit(solution)/shard_map/ppermute | solution.py:138
  186.6 6.0 %collective-permute-start.9 = (f32[8,2,32,512]{3,2,1,0:T(8,128)S(1)}, f32[8,2,32,512]{3,2,1,0:T(8,128)S(1)}, u32[]{:S(2)}, u32[]{:S(2)}) collective-permute-start(f32[8,2,32,512]{3,2,1,0:T(8,128)S(1)} %bitcast.43), channel_id=1, source_target_pairs={{0,1},{1,0},{2,3},{3,2},{4,5},{5,4},{6,7},{7,6},{8,9},{9,8},{10,11... | collective-permute-start | bytes 3145736 | tf_op jit(solution)/shard_map/ppermute | solution.py:152
  193.8 13.1 %collective-permute-start.10 = (f32[32,512]{1,0:T(8,128)S(1)}, f32[32,512]{1,0:T(8,128)S(1)}, u32[]{:S(2)}, u32[]{:S(2)}) collective-permute-start(f32[32,512]{1,0:T(8,128)S(1)} %shard_map.32), channel_id=1, source_target_pairs={{396,0},{428,1},{412,2},{444,3},{460,4},{492,5},{476,6},{508,7},{3... | collective-permute-start | bytes 196616 | tf_op jit(solution)/shard_map/ppermute | solution.py:35

commit v4 on v3

--- a/solution.py
+++ b/solution.py
@@ -10,14 +10,14 @@
 
 AXES = ("yh", "yl", "xh", "xl", "zh", "zl", "core")
 SIZES = (4, 2, 2, 2, 4, 2, 2)
-GROUP = ("yl", "xl", "xh")
+GROUP = ("xl", "zl", "xh")
 BLOCKS = 32
 LEVELS = 5
 
 
 def site(block):
     bit = [(block >> i) & 1 for i in range(5)]
-    return 2 * bit[2] + bit[1], 2 * bit[0] + bit[3], bit[4]
+    return 2 * bit[2] + bit[1], bit[4], 2 * bit[0] + bit[3]
 
 
 def origin(block, rows):
@@ -25,9 +25,9 @@
 
 
 def place(block, rows):
-    yh, zh, zl = site(block % BLOCKS)
+    yh, yl, zh = site(block % BLOCKS)
     core, chip = divmod(rows, 8)
-    return int(np.ravel_multi_index((yh, chip // 4, chip % 2, chip // 2 % 2, zh, zl, core), SIZES))
+    return int(np.ravel_multi_index((yh, yl, chip % 2, chip // 4, zh, chip // 2 % 2, core), SIZES))
 
 
 def move(array, source, target):
@@ -75,7 +75,7 @@
     return pieces[0] + pieces[1]
 
 
-def level_kernel(info, mine, theirs, term, later_map, out, sent, turned, twice):
+def level_kernel(before_last, info, mine, theirs, term, later_map, out, sent, turned, twice):
     core, column, counts = info[0], info[1], info[2]
     halves = (mine, theirs)
     left = rows_of_map(column, [lambda at, half=half: half[:, :, at] for half in halves], turned)
@@ -91,6 +91,10 @@
     left = jnp.concatenate([jnp.concatenate(weighted, 1), own_first(core, later_map[...])], 0)
     both = times(left, [half[:, :, :512] for half in halves])
     total = term[...] + jnp.where(counts != 0, both[:32], 0.0)
+    if before_last:
+        out[...] = total
+        sent[...] = jnp.where(info[3] != 0, both[32:], total)
+        return
     out[0] = both[32:]
     out[1] = total
     twice[:, :512] = total
@@ -120,9 +124,10 @@
 
 
 def local(local_term, coupling):
-    core, yh, zh, zl = (lax.axis_index(a) for a in ("core", "yh", "zh", "zl"))
+    core, yh, zh, yl = (lax.axis_index(a) for a in ("core", "yh", "zh", "yl"))
     column = core * 8 + lax.axis_index(GROUP)
-    end = zh // 2 + 2 * (yh % 2) + 4 * (yh // 2) + 8 * (zh % 2) + 16 * zl
+    end = zh // 2 + 2 * (yh % 2) + 4 * (yh // 2) + 8 * (zh % 2) + 16 * yl
+    is_earlier = (end - 15) % BLOCKS < 16
     both = jnp.concatenate([coupling, local_term], 0)
     for level in range(LEVELS - 1):
         length = 1 << level
@@ -137,22 +142,21 @@
         mine = lax.all_to_all(jnp.broadcast_to(rows[None], (8, 32, 896)), GROUP, 0, 0, tiled=True)
         theirs = lax.ppermute(mine, "core", [(0, 1), (1, 0)])
         counts = (end - 2 * length + 1) % BLOCKS + length < BLOCKS
+        before_last = level == LEVELS - 2
         both, sent = call(
-            level_kernel,
-            [(2, 32, 512), (32, 384)],
+            functools.partial(level_kernel, before_last),
+            [(32, 512), (32, 512)] if before_last else [(2, 32, 512), (32, 384)],
             [(128, 512), (32, 1024)],
-            [core, column, counts],
+            [core, column, counts, is_earlier],
             *(mine, theirs, earlier[1], own[0]),
         )
 
-    is_earlier = (end - 15) % BLOCKS < 16
-    rows = jnp.where(is_earlier, both[0], both[1])
-    mine = lax.all_to_all(jnp.broadcast_to(rows[None], (16, 32, 512)), GROUP + ("zl",), 0, 0, tiled=True)
+    mine = lax.all_to_all(jnp.broadcast_to(sent[None], (16, 32, 512)), GROUP + ("yl",), 0, 0, tiled=True)
     mine = mine.reshape(8, 2, 32, 512)
     theirs = lax.ppermute(mine, "core", [(0, 1), (1, 0)])
-    map_slot = jnp.where(is_earlier, zl, 1 - zl)
+    map_slot = jnp.where(is_earlier, yl, 1 - yl)
     info = [core, column, map_slot, 1 - map_slot, is_earlier]
-    (term,) = call(last_kernel, [(32, 512)], [(128, 512)], info, mine, theirs, both[1])
+    (term,) = call(last_kernel, [(32, 512)], [(128, 512)], info, mine, theirs, both)
     return move(term, lambda t, r: place(t + 15, r), origin)[None]
 
 

time: 208 us -> 205 us (0.986)
  waiting for transfers between devices: 61 us -> 47.1 us
  starting transfers between devices: 50.3 us -> 61.6 us
    ppermute x6, waiting for transfers between devices: 50.9 us -> 36.5 us  [move(): return lax.ppermute(array, AXES, pairs)]
    ppermute x6, starting transfers between devices: 30.1 us -> 41.6 us  [move(): return lax.ppermute(array, AXES, pairs)]
    all_to_all x4, blocking collectives: 66.9 us -> 69 us  [local(): lax.all_to_all(jnp.broadcast_to(rows[None], (8, 32, 896)), GROUP, 0, 0, t...]
where the time goes in v4:
time: 205 us; the launch traced here: 204 us
  blocking collectives  86.3 us (42%)
  starting transfers between devices  61.6 us (30%)
  waiting for transfers between devices  47.1 us (23%)
  Pallas kernels  6.75 us (3%)
  local copies, waits for them, and re-layouts  2.14 us (1%)
    all_to_all x4, blocking collectives, local(): lax.all_to_all(jnp.broadcast_to(rows[None], (8, 32, 896)), GROUP, 0, 0, t...  69 us
    ppermute x6, starting transfers between devices, move(): return lax.ppermute(array, AXES, pairs)  41.6 us
    ppermute x6, waiting for transfers between devices, move(): return lax.ppermute(array, AXES, pairs)  36.5 us
    ppermute x5, starting transfers between devices, local(): theirs = lax.ppermute(mine, 'core', [(0, 1), (1, 0)])  20 us
    all_to_all x1, blocking collectives, local(): lax.all_to_all(jnp.broadcast_to(sent[None], (16, 32, 512)), GROUP + ('yl'...  17.3 us
    ppermute x5, waiting for transfers between devices, local(): theirs = lax.ppermute(mine, 'core', [(0, 1), (1, 0)])  10.5 us
    pallas_call x5, Pallas kernels, call(): pl.pallas_call(kernel, out_shape=[jax.ShapeDtypeStruct(shape, jnp.float32...  6.75 us
  transfers between devices with their start and end apart: 11, of which 10 were waited for; matrix products, arithmetic and copies ran while one was open for 0% of the time, Pallas kernels for 0%

profile of v4, /device:TPU:1, one launch (start us, length us, event | category | flops | bytes accessed | tf_op | source)
XLA Modules:
  0.0 204.5 jit_solution(252174478351927099)
XLA Ops:
  0.0 0.9 constant_dynamic-update-slice_fusion.1
  0.9 6.0 %collective-permute-start.1 = (f32[2,32,512]{2,1,0:T(8,128)S(1)}, f32[2,32,512]{2,1,0:T(8,128)S(1)}, u32[]{:S(2)}, u32[]{:S(2)}) collective-permute-start(f32[2,32,512]{2,1,0:T(8,128)S(1)} %constant_dynamic-update-slice_fusion), channel_id=1, source_target_pairs={{0,0},{1,32},{2,2},{3,34},{4,16},{5,48},{6,18},{7,50},{8,1},{9,33}... | collective-permute-start | bytes 393224 | tf_op jit(solution)/shard_map/ppermute | solution.py:35
  6.9 10.4 %collective-permute-start = (f32[2,32,512]{2,1,0:T(8,128)S(1)}, f32[2,32,512]{2,1,0:T(8,128)S(1)}, u32[]{:S(2)}, u32[]{:S(2)}) collective-permute-start(f32[2,32,512]{2,1,0:T(8,128)S(1)} %constant_dynamic-update-slice_fusion), channel_id=1, source_target_pairs={{0,8},{1,40},{2,10},{3,42},{4,24},{5,56},{6,26},{7,58},{8,9},{9,41... | collective-permute-start | bytes 393224 | tf_op jit(solution)/shard_map/ppermute | solution.py:35
  17.5 9.3 %collective-permute-done = f32[2,32,512]{2,1,0:T(8,128)S(1)} collective-permute-done((f32[2,32,512]{2,1,0:T(8,128)S(1)}, f32[2,32,512]{2,1,0:T(8,128)S(1)}, u32[]{:S(2)}, u32[]{:S(2)}) %collective-permute-start) | collective-permute-done | bytes 131104 | tf_op jit(solution)/shard_map/ppermute | solution.py:35
  26.9 23.2 %all_to_all.25.mine = f32[8,32,896]{2,1,0:T(8,128)S(1)} all-to-all(f32[8,32,896]{2,1,0:T(8,128)S(1)} %broadcast_in_dim.12), channel_id=1, replica_groups=mesh['yh'=4,'yl'=2,'xh'=2,'xl'=2,'zh'=4,'zl'=2,'core'=2] {'xl','zl','xh'}, dimensions={0} | all-to-all | bytes 1835008 | tf_op jit(solution)/shard_map/all_to_all | solution.py:142
  50.1 1.9 collective-permute-start.2
  52.2 2.3 %collective-permute-done.2.theirs = f32[8,32,896]{2,1,0:T(8,128)S(1)} collective-permute-done((f32[8,32,896]{2,1,0:T(8,128)S(1)}, f32[8,32,896]{2,1,0:T(8,128)S(1)}, u32[]{:S(2)}, u32[]{:S(2)}) %collective-permute-start.2) | collective-permute-done | bytes 917536 | tf_op jit(solution)/shard_map/ppermute | solution.py:143
  54.4 1.4 shard_map.28
  55.8 3.8 %collective-permute-start.3 = (f32[2,32,512]{2,1,0:T(8,128)S(1)}, f32[2,32,512]{2,1,0:T(8,128)S(1)}, u32[]{:S(2)}, u32[]{:S(2)}) collective-permute-start(f32[2,32,512]{2,1,0:T(8,128)S(1)} %get-tuple-element.13), channel_id=1, source_target_pairs={{0,128},{32,160},{2,130},{34,162},{16,144},{48,176},{18,146},{50,1... | collective-permute-start | bytes 393224 | tf_op jit(solution)/shard_map/ppermute | solution.py:35
  59.6 7.5 %collective-permute-done.3 = f32[2,32,512]{2,1,0:T(8,128)S(1)} collective-permute-done((f32[2,32,512]{2,1,0:T(8,128)S(1)}, f32[2,32,512]{2,1,0:T(8,128)S(1)}, u32[]{:S(2)}, u32[]{:S(2)}) %collective-permute-start.3) | collective-permute-done | bytes 131104 | tf_op jit(solution)/shard_map/ppermute | solution.py:35
  67.3 15.5 %all_to_all.26.mine = f32[8,32,896]{2,1,0:T(8,128)S(1)} all-to-all(f32[8,32,896]{2,1,0:T(8,128)S(1)} %broadcast_in_dim.13), channel_id=1, replica_groups=mesh['yh'=4,'yl'=2,'xh'=2,'xl'=2,'zh'=4,'zl'=2,'core'=2] {'xl','zl','xh'}, dimensions={0} | all-to-all | bytes 1835008 | tf_op jit(solution)/shard_map/all_to_all | solution.py:142
  82.7 4.6 %collective-permute-start.4 = (f32[8,32,896]{2,1,0:T(8,128)S(1)}, f32[8,32,896]{2,1,0:T(8,128)S(1)}, u32[]{:S(2)}, u32[]{:S(2)}) collective-permute-start(f32[8,32,896]{2,1,0:T(8,128)S(1)} %all_to_all.26.mine), channel_id=1, source_target_pairs={{0,1},{1,0},{2,3},{3,2},{4,5},{5,4},{6,7},{7,6},{8,9},{9,8},{10,11... | collective-permute-start | bytes 2752520 | tf_op jit(solution)/shard_map/ppermute | solution.py:143
  87.4 1.9 collective-permute-done.4.theirs
  89.4 1.4 shard_map.29
  90.8 7.4 %collective-permute-start.5 = (f32[2,32,512]{2,1,0:T(8,128)S(1)}, f32[2,32,512]{2,1,0:T(8,128)S(1)}, u32[]{:S(2)}, u32[]{:S(2)}) collective-permute-start(f32[2,32,512]{2,1,0:T(8,128)S(1)} %get-tuple-element.15), channel_id=1, source_target_pairs={{0,256},{32,288},{2,258},{34,290},{16,272},{48,304},{18,274},{50,3... | collective-permute-start | bytes 393224 | tf_op jit(solution)/shard_map/ppermute | solution.py:35
  98.2 5.4 %collective-permute-done.5 = f32[2,32,512]{2,1,0:T(8,128)S(1)} collective-permute-done((f32[2,32,512]{2,1,0:T(8,128)S(1)}, f32[2,32,512]{2,1,0:T(8,128)S(1)}, u32[]{:S(2)}, u32[]{:S(2)}) %collective-permute-start.5) | collective-permute-done | bytes 131104 | tf_op jit(solution)/shard_map/ppermute | solution.py:35
  103.7 15.0 %all_to_all.27.mine = f32[8,32,896]{2,1,0:T(8,128)S(1)} all-to-all(f32[8,32,896]{2,1,0:T(8,128)S(1)} %broadcast_in_dim.14), channel_id=1, replica_groups=mesh['yh'=4,'yl'=2,'xh'=2,'xl'=2,'zh'=4,'zl'=2,'core'=2] {'xl','zl','xh'}, dimensions={0} | all-to-all | bytes 1835008 | tf_op jit(solution)/shard_map/all_to_all | solution.py:142
  118.7 5.0 %collective-permute-start.6 = (f32[8,32,896]{2,1,0:T(8,128)S(1)}, f32[8,32,896]{2,1,0:T(8,128)S(1)}, u32[]{:S(2)}, u32[]{:S(2)}) collective-permute-start(f32[8,32,896]{2,1,0:T(8,128)S(1)} %all_to_all.27.mine), channel_id=1, source_target_pairs={{0,1},{1,0},{2,3},{3,2},{4,5},{5,4},{6,7},{7,6},{8,9},{9,8},{10,11... | collective-permute-start | bytes 2752520 | tf_op jit(solution)/shard_map/ppermute | solution.py:143
  123.8 2.1 %collective-permute-done.6.theirs = f32[8,32,896]{2,1,0:T(8,128)S(1)} collective-permute-done((f32[8,32,896]{2,1,0:T(8,128)S(1)}, f32[8,32,896]{2,1,0:T(8,128)S(1)}, u32[]{:S(2)}, u32[]{:S(2)}) %collective-permute-start.6) | collective-permute-done | bytes 917536 | tf_op jit(solution)/shard_map/ppermute | solution.py:143
  125.8 1.4 shard_map.30
  127.2 9.2 %collective-permute-start.7 = (f32[2,32,512]{2,1,0:T(8,128)S(1)}, f32[2,32,512]{2,1,0:T(8,128)S(1)}, u32[]{:S(2)}, u32[]{:S(2)}) collective-permute-start(f32[2,32,512]{2,1,0:T(8,128)S(1)} %get-tuple-element.17), channel_id=1, source_target_pairs={{0,4},{32,36},{2,6},{34,38},{16,20},{48,52},{18,22},{50,54},{1,5},... | collective-permute-start | bytes 393224 | tf_op jit(solution)/shard_map/ppermute | solution.py:35
  136.4 5.4 %collective-permute-done.7 = f32[2,32,512]{2,1,0:T(8,128)S(1)} collective-permute-done((f32[2,32,512]{2,1,0:T(8,128)S(1)}, f32[2,32,512]{2,1,0:T(8,128)S(1)}, u32[]{:S(2)}, u32[]{:S(2)}) %collective-permute-start.7) | collective-permute-done | bytes 131104 | tf_op jit(solution)/shard_map/ppermute | solution.py:35
  141.9 15.3 %all_to_all.28.mine = f32[8,32,896]{2,1,0:T(8,128)S(1)} all-to-all(f32[8,32,896]{2,1,0:T(8,128)S(1)} %broadcast_in_dim.15), channel_id=1, replica_groups=mesh['yh'=4,'yl'=2,'xh'=2,'xl'=2,'zh'=4,'zl'=2,'core'=2] {'xl','zl','xh'}, dimensions={0} | all-to-all | bytes 1835008 | tf_op jit(solution)/shard_map/all_to_all | solution.py:142
  157.2 4.4 %collective-permute-start.8 = (f32[8,32,896]{2,1,0:T(8,128)S(1)}, f32[8,32,896]{2,1,0:T(8,128)S(1)}, u32[]{:S(2)}, u32[]{:S(2)}) collective-permute-start(f32[8,32,896]{2,1,0:T(8,128)S(1)} %all_to_all.28.mine), channel_id=1, source_target_pairs={{0,1},{1,0},{2,3},{3,2},{4,5},{5,4},{6,7},{7,6},{8,9},{9,8},{10,11... | collective-permute-start | bytes 2752520 | tf_op jit(solution)/shard_map/ppermute | solution.py:143
  161.7 2.1 %collective-permute-done.8.theirs = f32[8,32,896]{2,1,0:T(8,128)S(1)} collective-permute-done((f32[8,32,896]{2,1,0:T(8,128)S(1)}, f32[8,32,896]{2,1,0:T(8,128)S(1)}, u32[]{:S(2)}, u32[]{:S(2)}) %collective-permute-start.8) | collective-permute-done | bytes 917536 | tf_op jit(solution)/shard_map/ppermute | solution.py:143
  163.8 1.4 shard_map.31
  165.3 17.3 %all_to_all.29 = f32[16,32,512]{2,1,0:T(8,128)S(1)} all-to-all(f32[16,32,512]{2,1,0:T(8,128)S(1)} %broadcast_in_dim.16), channel_id=1, replica_groups=mesh['yh'=4,'yl'=2,'xh'=2,'xl'=2,'zh'=4,'zl'=2,'core'=2] {'xl','zl','xh'..., dimensions={0} | all-to-all | bytes 2097152 | tf_op jit(solution)/shard_map/all_to_all | solution.py:154
  182.6 4.1 %collective-permute-start.9 = (f32[8,2,32,512]{3,2,1,0:T(8,128)S(1)}, f32[8,2,32,512]{3,2,1,0:T(8,128)S(1)}, u32[]{:S(2)}, u32[]{:S(2)}) collective-permute-start(f32[8,2,32,512]{3,2,1,0:T(8,128)S(1)} %bitcast.39), channel_id=1, source_target_pairs={{0,1},{1,0},{2,3},{3,2},{4,5},{5,4},{6,7},{7,6},{8,9},{9,8},{10,11... | collective-permute-start | bytes 3145736 | tf_op jit(solution)/shard_map/ppermute | solution.py:156
  186.8 2.2 %collective-permute-done.9.theirs = f32[8,2,32,512]{3,2,1,0:T(8,128)S(1)} collective-permute-done((f32[8,2,32,512]{3,2,1,0:T(8,128)S(1)}, f32[8,2,32,512]{3,2,1,0:T(8,128)S(1)}, u32[]{:S(2)}, u32[]{:S(2)}) %collective-permute-start.9) | collective-permute-done | bytes 1048608 | tf_op jit(solution)/shard_map/ppermute | solution.py:156
  188.9 1.2 shard_map.32
  190.2 4.8 %collective-permute-start.10 = (f32[32,512]{1,0:T(8,128)S(1)}, f32[32,512]{1,0:T(8,128)S(1)}, u32[]{:S(2)}, u32[]{:S(2)}) collective-permute-start(f32[32,512]{1,0:T(8,128)S(1)} %shard_map.32), channel_id=1, source_target_pairs={{396,0},{428,1},{398,2},{430,3},{412,4},{444,5},{414,6},{446,7},{3... | collective-permute-start | bytes 196616 | tf_op jit(solution)/shard_map/ppermute | solution.py:35
  195.0 8.9 %collective-permute-done.10 = f32[32,512]{1,0:T(8,128)S(1)} collective-permute-done((f32[32,512]{1,0:T(8,128)S(1)}, f32[32,512]{1,0:T(8,128)S(1)}, u32[]{:S(2)}, u32[]{:S(2)}) %collective-permute-start.10) | collective-permute-done | bytes 65568 | tf_op jit(solution)/shard_map/ppermute | solution.py:35
  (28 shorter events, 1.5 us)
Async XLA Ops:
  0.0 0.9 copy-start
  0.9 16.5 %collective-permute-start.1 = (f32[2,32,512]{2,1,0:T(8,128)S(1)}, f32[2,32,512]{2,1,0:T(8,128)S(1)}, u32[]{:S(2)}, u32[]{:S(2)}) collective-permute-start(f32[2,32,512]{2,1,0:T(8,128)S(1)} %constant_dynamic-update-slice_fusion), channel_id=1, source_target_pairs={{0,0},{1,32},{2,2},{3,34},{4,16},{5,48},{6,18},{7,50},{8,1},{9,33}... | collective-permute-start | bytes 393224 | tf_op jit(solution)/shard_map/ppermute | solution.py:35
  6.9 19.8 %collective-permute-start = (f32[2,32,512]{2,1,0:T(8,128)S(1)}, f32[2,32,512]{2,1,0:T(8,128)S(1)}, u32[]{:S(2)}, u32[]{:S(2)}) collective-permute-start(f32[2,32,512]{2,1,0:T(8,128)S(1)} %constant_dynamic-update-slice_fusion), channel_id=1, source_target_pairs={{0,8},{1,40},{2,10},{3,42},{4,24},{5,56},{6,26},{7,58},{8,9},{9,41... | collective-permute-start | bytes 393224 | tf_op jit(solution)/shard_map/ppermute | solution.py:35
  50.1 4.4 %collective-permute-start.2 = (f32[8,32,896]{2,1,0:T(8,128)S(1)}, f32[8,32,896]{2,1,0:T(8,128)S(1)}, u32[]{:S(2)}, u32[]{:S(2)}) collective-permute-start(f32[8,32,896]{2,1,0:T(8,128)S(1)} %all_to_all.25.mine), channel_id=1, source_target_pairs={{0,1},{1,0},{2,3},{3,2},{4,5},{5,4},{6,7},{7,6},{8,9},{9,8},{10,11... | collective-permute-start | bytes 2752520 | tf_op jit(solution)/shard_map/ppermute | solution.py:143
  55.8 11.3 %collective-permute-start.3 = (f32[2,32,512]{2,1,0:T(8,128)S(1)}, f32[2,32,512]{2,1,0:T(8,128)S(1)}, u32[]{:S(2)}, u32[]{:S(2)}) collective-permute-start(f32[2,32,512]{2,1,0:T(8,128)S(1)} %get-tuple-element.13), channel_id=1, source_target_pairs={{0,128},{32,160},{2,130},{34,162},{16,144},{48,176},{18,146},{50,1... | collective-permute-start | bytes 393224 | tf_op jit(solution)/shard_map/ppermute | solution.py:35
  82.7 6.7 %collective-permute-start.4 = (f32[8,32,896]{2,1,0:T(8,128)S(1)}, f32[8,32,896]{2,1,0:T(8,128)S(1)}, u32[]{:S(2)}, u32[]{:S(2)}) collective-permute-start(f32[8,32,896]{2,1,0:T(8,128)S(1)} %all_to_all.26.mine), channel_id=1, source_target_pairs={{0,1},{1,0},{2,3},{3,2},{4,5},{5,4},{6,7},{7,6},{8,9},{9,8},{10,11... | collective-permute-start | bytes 2752520 | tf_op jit(solution)/shard_map/ppermute | solution.py:143
  90.8 12.8 %collective-permute-start.5 = (f32[2,32,512]{2,1,0:T(8,128)S(1)}, f32[2,32,512]{2,1,0:T(8,128)S(1)}, u32[]{:S(2)}, u32[]{:S(2)}) collective-permute-start(f32[2,32,512]{2,1,0:T(8,128)S(1)} %get-tuple-element.15), channel_id=1, source_target_pairs={{0,256},{32,288},{2,258},{34,290},{16,272},{48,304},{18,274},{50,3... | collective-permute-start | bytes 393224 | tf_op jit(solution)/shard_map/ppermute | solution.py:35
  118.7 7.1 %collective-permute-start.6 = (f32[8,32,896]{2,1,0:T(8,128)S(1)}, f32[8,32,896]{2,1,0:T(8,128)S(1)}, u32[]{:S(2)}, u32[]{:S(2)}) collective-permute-start(f32[8,32,896]{2,1,0:T(8,128)S(1)} %all_to_all.27.mine), channel_id=1, source_target_pairs={{0,1},{1,0},{2,3},{3,2},{4,5},{5,4},{6,7},{7,6},{8,9},{9,8},{10,11... | collective-permute-start | bytes 2752520 | tf_op jit(solution)/shard_map/ppermute | solution.py:143
  127.2 14.6 %collective-permute-start.7 = (f32[2,32,512]{2,1,0:T(8,128)S(1)}, f32[2,32,512]{2,1,0:T(8,128)S(1)}, u32[]{:S(2)}, u32[]{:S(2)}) collective-permute-start(f32[2,32,512]{2,1,0:T(8,128)S(1)} %get-tuple-element.17), channel_id=1, source_target_pairs={{0,4},{32,36},{2,6},{34,38},{16,20},{48,52},{18,22},{50,54},{1,5},... | collective-permute-start | bytes 393224 | tf_op jit(solution)/shard_map/ppermute | solution.py:35
  157.2 6.5 %collective-permute-start.8 = (f32[8,32,896]{2,1,0:T(8,128)S(1)}, f32[8,32,896]{2,1,0:T(8,128)S(1)}, u32[]{:S(2)}, u32[]{:S(2)}) collective-permute-start(f32[8,32,896]{2,1,0:T(8,128)S(1)} %all_to_all.28.mine), channel_id=1, source_target_pairs={{0,1},{1,0},{2,3},{3,2},{4,5},{5,4},{6,7},{7,6},{8,9},{9,8},{10,11... | collective-permute-start | bytes 2752520 | tf_op jit(solution)/shard_map/ppermute | solution.py:143
  182.6 6.3 %collective-permute-start.9 = (f32[8,2,32,512]{3,2,1,0:T(8,128)S(1)}, f32[8,2,32,512]{3,2,1,0:T(8,128)S(1)}, u32[]{:S(2)}, u32[]{:S(2)}) collective-permute-start(f32[8,2,32,512]{3,2,1,0:T(8,128)S(1)} %bitcast.39), channel_id=1, source_target_pairs={{0,1},{1,0},{2,3},{3,2},{4,5},{5,4},{6,7},{7,6},{8,9},{9,8},{10,11... | collective-permute-start | bytes 3145736 | tf_op jit(solution)/shard_map/ppermute | solution.py:156
  190.2 13.7 %collective-permute-start.10 = (f32[32,512]{1,0:T(8,128)S(1)}, f32[32,512]{1,0:T(8,128)S(1)}, u32[]{:S(2)}, u32[]{:S(2)}) collective-permute-start(f32[32,512]{1,0:T(8,128)S(1)} %shard_map.32), channel_id=1, source_target_pairs={{396,0},{428,1},{398,2},{430,3},{412,4},{444,5},{414,6},{446,7},{3... | collective-permute-start | bytes 196616 | tf_op jit(solution)/shard_map/ppermute | solution.py:35

commit v5 on v4

--- a/solution.py
+++ b/solution.py
@@ -61,7 +61,7 @@
     slab = pl.ds(pl.multiple_of((column // 4) * 128, 128), 128)
     for i, half in enumerate(halves):
         turned[:, 256 * i : 256 * i + 256] = half(slab).reshape(256, 128).T
-    return turned[pl.ds(pl.multiple_of((column % 4) * 32, 32), 32), :]
+    return turned[pl.ds(pl.multiple_of((column % 4) * 32, 32), 32), : 256 * len(halves)]
 
 
 def own_first(core, rows):
@@ -75,27 +75,49 @@
     return pieces[0] + pieces[1]
 
 
-def level_kernel(before_last, info, mine, theirs, term, later_map, out, sent, turned, twice):
-    core, column, counts = info[0], info[1], info[2]
-    halves = (mine, theirs)
-    left = rows_of_map(column, [lambda at, half=half: half[:, :, at] for half in halves], turned)
-    lefts = [split(left[:, 128 * i : 128 * i + 128]) for i in range(4)]
-    stored = blocks(halves, 512, 384)
+def early_kernel(info, mine, later_map, out_left, out_weighted, out_map, turned):
+    core, column = info[0], info[1]
+    left = rows_of_map(column, [lambda at: mine[:, :, at]], turned)
+    lefts = [split(left[:, 128 * i : 128 * i + 128]) for i in range(2)]
+    stored = blocks([mine], 512, 384)
     weighted = [0.0] * 4
-    for i in range(4):
+    for i in range(2):
         row = product(lefts[i], stored[i])
         for j in range(3):
+            weighted[i + j] += row[:, 128 * j : 128 * j + 128]
+    weighted[0] += product(lefts[1], tuple(part[:, 128:256] for part in stored[0]), True)
+    out_left[...] = left
+    out_weighted[...] = jnp.concatenate(weighted, 1)
+    own = own_first(core, later_map[...])[:, :256]
+    out_map[...] = product(split(own), split(mine[:, :, :512].reshape(256, 512)))
+
+
+def level_kernel(before_last, info, mine, theirs, term, later_map, early_left, early_weighted, early_map, out, sent, turned, twice):
+    core, column, counts = info[0], info[1], info[2]
+    left = jnp.concatenate([early_left[...], rows_of_map(column, [lambda at: theirs[:, :, at]], turned)], 1)
+    lefts = [split(left[:, 128 * i : 128 * i + 128]) for i in range(4)]
+    stored = blocks([theirs], 512, 384)
+    weighted = [early_weighted[:, 128 * i : 128 * i + 128] for i in range(4)]
+    for i in (2, 3):
+        row = product(lefts[i], stored[i - 2])
+        for j in range(3):
             weighted[(i + j) % 4] += row[:, 128 * j : 128 * j + 128]
-        above = tuple(part[:, 128:256] for part in stored[i])
+    high, low = split(mine[4:, :, 640:768].reshape(128, 128))
+    weighted[1] += product(lefts[2], (high, low), True)
+    for i in (2, 3):
+        above = tuple(part[:, 128:256] for part in stored[i - 2])
         weighted[i] += product(lefts[(i + 1) % 4], above, True)
-    left = jnp.concatenate([jnp.concatenate(weighted, 1), own_first(core, later_map[...])], 0)
-    both = times(left, [half[:, :, :512] for half in halves])
-    total = term[...] + jnp.where(counts != 0, both[:32], 0.0)
+    own = jnp.concatenate(weighted[:2], 1)
+    other = jnp.concatenate([jnp.concatenate(weighted[2:], 1), own_first(core, later_map[...])[:, 256:]], 0)
+    total = product(split(own), split(mine[:, :, :512].reshape(256, 512)))
+    both = product(split(other), split(theirs[:, :, :512].reshape(256, 512)))
+    total = term[...] + jnp.where(counts != 0, total + both[:32], 0.0)
+    new_map = early_map[...] + both[32:]
     if before_last:
         out[...] = total
-        sent[...] = jnp.where(info[3] != 0, both[32:], total)
+        sent[...] = jnp.where(info[3] != 0, new_map, total)
         return
-    out[0] = both[32:]
+    out[0] = new_map
     out[1] = total
     twice[:, :512] = total
     twice[:, 512:] = total
@@ -143,12 +165,16 @@
         theirs = lax.ppermute(mine, "core", [(0, 1), (1, 0)])
         counts = (end - 2 * length + 1) % BLOCKS + length < BLOCKS
         before_last = level == LEVELS - 2
+        info = [core, column, counts, is_earlier]
+        early = call(
+            early_kernel, [(32, 256), (32, 512), (32, 512)], [(128, 256)], info, mine, own[0]
+        )
         both, sent = call(
             functools.partial(level_kernel, before_last),
             [(32, 512), (32, 512)] if before_last else [(2, 32, 512), (32, 384)],
-            [(128, 512), (32, 1024)],
-            [core, column, counts, is_earlier],
-            *(mine, theirs, earlier[1], own[0]),
+            [(128, 256), (32, 1024)],
+            info,
+            *(mine, theirs, earlier[1], own[0], *early),
         )
 
     mine = lax.all_to_all(jnp.broadcast_to(sent[None], (16, 32, 512)), GROUP + ("yl",), 0, 0, tiled=True)

time: 205 us -> 205 us (level)
  waiting for transfers between devices: 47.1 us -> 43.2 us
  Pallas kernels: 6.75 us -> 10.1 us
    ppermute x5, waiting for transfers between devices: 10.5 us -> 6.65 us  [local(): theirs = lax.ppermute(mine, 'core', [(0, 1), (1, 0)])]
    pallas_call x5 -> x9, Pallas kernels: 6.75 us -> 10.1 us  [call(): pl.pallas_call(kernel, out_shape=[jax.ShapeDtypeStruct(shape, jnp.float32...]
  transfers between devices with their start and end apart: 11 -> 11, of which waited for: 10 -> 10; matrix products, arithmetic and copies ran while one was open for 0% -> 0% of each run, Pallas kernels for 0% -> 2%
where the time goes in v5:
time: 205 us; the launch traced here: 204 us
  blocking collectives  86.4 us (42%)
  starting transfers between devices  61.5 us (30%)
  waiting for transfers between devices  43.2 us (21%)
  Pallas kernels  10.1 us (5%)
  local copies, waits for them, and re-layouts  2.14 us (1%)
    all_to_all x4, blocking collectives, local(): lax.all_to_all(jnp.broadcast_to(rows[None], (8, 32, 896)), GROUP, 0, 0, t...  69 us
    ppermute x6, starting transfers between devices, move(): return lax.ppermute(array, AXES, pairs)  41.6 us
    ppermute x6, waiting for transfers between devices, move(): return lax.ppermute(array, AXES, pairs)  36.5 us
    ppermute x5, starting transfers between devices, local(): theirs = lax.ppermute(mine, 'core', [(0, 1), (1, 0)])  20 us
    all_to_all x1, blocking collectives, local(): lax.all_to_all(jnp.broadcast_to(sent[None], (16, 32, 512)), GROUP + ('yl'...  17.4 us
    pallas_call x9, Pallas kernels, call(): pl.pallas_call(kernel, out_shape=[jax.ShapeDtypeStruct(shape, jnp.float32...  10.1 us
    ppermute x5, waiting for transfers between devices, local(): theirs = lax.ppermute(mine, 'core', [(0, 1), (1, 0)])  6.65 us
  transfers between devices with their start and end apart: 11, of which 10 were waited for; matrix products, arithmetic and copies ran while one was open for 0% of the time, Pallas kernels for 2%

profile of v5, /device:TPU:1, one launch (start us, length us, event | category | flops | bytes accessed | tf_op | source)
XLA Modules:
  0.0 204.1 jit_solution(9694939691479010342)
XLA Ops:
  0.9 6.0 %collective-permute-start.1 = (f32[2,32,512]{2,1,0:T(8,128)S(1)}, f32[2,32,512]{2,1,0:T(8,128)S(1)}, u32[]{:S(2)}, u32[]{:S(2)}) collective-permute-start(f32[2,32,512]{2,1,0:T(8,128)S(1)} %constant_dynamic-update-slice_fusion), channel_id=1, source_target_pairs={{0,0},{1,32},{2,2},{3,34},{4,16},{5,48},{6,18},{7,50},{8,1},{9,33}... | collective-permute-start | bytes 393224 | tf_op jit(solution)/shard_map/ppermute | solution.py:35
  6.9 10.4 %collective-permute-start = (f32[2,32,512]{2,1,0:T(8,128)S(1)}, f32[2,32,512]{2,1,0:T(8,128)S(1)}, u32[]{:S(2)}, u32[]{:S(2)}) collective-permute-start(f32[2,32,512]{2,1,0:T(8,128)S(1)} %constant_dynamic-update-slice_fusion), channel_id=1, source_target_pairs={{0,8},{1,40},{2,10},{3,42},{4,24},{5,56},{6,26},{7,58},{8,9},{9,41... | collective-permute-start | bytes 393224 | tf_op jit(solution)/shard_map/ppermute | solution.py:35
  17.5 9.3 %collective-permute-done = f32[2,32,512]{2,1,0:T(8,128)S(1)} collective-permute-done((f32[2,32,512]{2,1,0:T(8,128)S(1)}, f32[2,32,512]{2,1,0:T(8,128)S(1)}, u32[]{:S(2)}, u32[]{:S(2)}) %collective-permute-start) | collective-permute-done | bytes 131104 | tf_op jit(solution)/shard_map/ppermute | solution.py:35
  26.9 23.2 %all_to_all.25.mine = f32[8,32,896]{2,1,0:T(8,128)S(1)} all-to-all(f32[8,32,896]{2,1,0:T(8,128)S(1)} %broadcast_in_dim.12), channel_id=1, replica_groups=mesh['yh'=4,'yl'=2,'xh'=2,'xl'=2,'zh'=4,'zl'=2,'core'=2] {'xl','zl','xh'}, dimensions={0} | all-to-all | bytes 1835008 | tf_op jit(solution)/shard_map/all_to_all | solution.py:164
  50.1 1.9 collective-permute-start.2
  53.1 1.3 collective-permute-done.2.theirs
  54.4 1.3 shard_map.29
  55.7 3.8 %collective-permute-start.3 = (f32[2,32,512]{2,1,0:T(8,128)S(1)}, f32[2,32,512]{2,1,0:T(8,128)S(1)}, u32[]{:S(2)}, u32[]{:S(2)}) collective-permute-start(f32[2,32,512]{2,1,0:T(8,128)S(1)} %get-tuple-element.28), channel_id=1, source_target_pairs={{0,128},{32,160},{2,130},{34,162},{16,144},{48,176},{18,146},{50,1... | collective-permute-start | bytes 393224 | tf_op jit(solution)/shard_map/ppermute | solution.py:35
  59.5 7.5 %collective-permute-done.3 = f32[2,32,512]{2,1,0:T(8,128)S(1)} collective-permute-done((f32[2,32,512]{2,1,0:T(8,128)S(1)}, f32[2,32,512]{2,1,0:T(8,128)S(1)}, u32[]{:S(2)}, u32[]{:S(2)}) %collective-permute-start.3) | collective-permute-done | bytes 131104 | tf_op jit(solution)/shard_map/ppermute | solution.py:35
  67.1 15.5 %all_to_all.26.mine = f32[8,32,896]{2,1,0:T(8,128)S(1)} all-to-all(f32[8,32,896]{2,1,0:T(8,128)S(1)} %broadcast_in_dim.13), channel_id=1, replica_groups=mesh['yh'=4,'yl'=2,'xh'=2,'xl'=2,'zh'=4,'zl'=2,'core'=2] {'xl','zl','xh'}, dimensions={0} | all-to-all | bytes 1835008 | tf_op jit(solution)/shard_map/all_to_all | solution.py:164
  82.6 4.6 %collective-permute-start.4 = (f32[8,32,896]{2,1,0:T(8,128)S(1)}, f32[8,32,896]{2,1,0:T(8,128)S(1)}, u32[]{:S(2)}, u32[]{:S(2)}) collective-permute-start(f32[8,32,896]{2,1,0:T(8,128)S(1)} %all_to_all.26.mine), channel_id=1, source_target_pairs={{0,1},{1,0},{2,3},{3,2},{4,5},{5,4},{6,7},{7,6},{8,9},{9,8},{10,11... | collective-permute-start | bytes 2752520 | tf_op jit(solution)/shard_map/ppermute | solution.py:165
  88.3 1.0 collective-permute-done.4.theirs
  89.3 1.3 shard_map.31
  90.6 7.4 %collective-permute-start.5 = (f32[2,32,512]{2,1,0:T(8,128)S(1)}, f32[2,32,512]{2,1,0:T(8,128)S(1)}, u32[]{:S(2)}, u32[]{:S(2)}) collective-permute-start(f32[2,32,512]{2,1,0:T(8,128)S(1)} %get-tuple-element.33), channel_id=1, source_target_pairs={{0,256},{32,288},{2,258},{34,290},{16,272},{48,304},{18,274},{50,3... | collective-permute-start | bytes 393224 | tf_op jit(solution)/shard_map/ppermute | solution.py:35
  98.0 5.4 %collective-permute-done.5 = f32[2,32,512]{2,1,0:T(8,128)S(1)} collective-permute-done((f32[2,32,512]{2,1,0:T(8,128)S(1)}, f32[2,32,512]{2,1,0:T(8,128)S(1)}, u32[]{:S(2)}, u32[]{:S(2)}) %collective-permute-start.5) | collective-permute-done | bytes 131104 | tf_op jit(solution)/shard_map/ppermute | solution.py:35
  103.5 15.1 %all_to_all.27.mine = f32[8,32,896]{2,1,0:T(8,128)S(1)} all-to-all(f32[8,32,896]{2,1,0:T(8,128)S(1)} %broadcast_in_dim.14), channel_id=1, replica_groups=mesh['yh'=4,'yl'=2,'xh'=2,'xl'=2,'zh'=4,'zl'=2,'core'=2] {'xl','zl','xh'}, dimensions={0} | all-to-all | bytes 1835008 | tf_op jit(solution)/shard_map/all_to_all | solution.py:164
  118.5 5.0 %collective-permute-start.6 = (f32[8,32,896]{2,1,0:T(8,128)S(1)}, f32[8,32,896]{2,1,0:T(8,128)S(1)}, u32[]{:S(2)}, u32[]{:S(2)}) collective-permute-start(f32[8,32,896]{2,1,0:T(8,128)S(1)} %all_to_all.27.mine), channel_id=1, source_target_pairs={{0,1},{1,0},{2,3},{3,2},{4,5},{5,4},{6,7},{7,6},{8,9},{9,8},{10,11... | collective-permute-start | bytes 2752520 | tf_op jit(solution)/shard_map/ppermute | solution.py:165
  124.5 1.1 collective-permute-done.6.theirs
  125.6 1.3 shard_map.33
  126.9 9.2 %collective-permute-start.7 = (f32[2,32,512]{2,1,0:T(8,128)S(1)}, f32[2,32,512]{2,1,0:T(8,128)S(1)}, u32[]{:S(2)}, u32[]{:S(2)}) collective-permute-start(f32[2,32,512]{2,1,0:T(8,128)S(1)} %get-tuple-element.38), channel_id=1, source_target_pairs={{0,4},{32,36},{2,6},{34,38},{16,20},{48,52},{18,22},{50,54},{1,5},... | collective-permute-start | bytes 393224 | tf_op jit(solution)/shard_map/ppermute | solution.py:35
  136.1 5.4 %collective-permute-done.7 = f32[2,32,512]{2,1,0:T(8,128)S(1)} collective-permute-done((f32[2,32,512]{2,1,0:T(8,128)S(1)}, f32[2,32,512]{2,1,0:T(8,128)S(1)}, u32[]{:S(2)}, u32[]{:S(2)}) %collective-permute-start.7) | collective-permute-done | bytes 131104 | tf_op jit(solution)/shard_map/ppermute | solution.py:35
  141.6 15.3 %all_to_all.28.mine = f32[8,32,896]{2,1,0:T(8,128)S(1)} all-to-all(f32[8,32,896]{2,1,0:T(8,128)S(1)} %broadcast_in_dim.15), channel_id=1, replica_groups=mesh['yh'=4,'yl'=2,'xh'=2,'xl'=2,'zh'=4,'zl'=2,'core'=2] {'xl','zl','xh'}, dimensions={0} | all-to-all | bytes 1835008 | tf_op jit(solution)/shard_map/all_to_all | solution.py:164
  156.9 4.4 %collective-permute-start.8 = (f32[8,32,896]{2,1,0:T(8,128)S(1)}, f32[8,32,896]{2,1,0:T(8,128)S(1)}, u32[]{:S(2)}, u32[]{:S(2)}) collective-permute-start(f32[8,32,896]{2,1,0:T(8,128)S(1)} %all_to_all.28.mine), channel_id=1, source_target_pairs={{0,1},{1,0},{2,3},{3,2},{4,5},{5,4},{6,7},{7,6},{8,9},{9,8},{10,11... | collective-permute-start | bytes 2752520 | tf_op jit(solution)/shard_map/ppermute | solution.py:165
  161.4 1.0 shard_map.34
  162.3 1.1 collective-permute-done.8.theirs
  163.4 1.3 shard_map.35
  164.8 17.4 %all_to_all.29 = f32[16,32,512]{2,1,0:T(8,128)S(1)} all-to-all(f32[16,32,512]{2,1,0:T(8,128)S(1)} %broadcast_in_dim.16), channel_id=1, replica_groups=mesh['yh'=4,'yl'=2,'xh'=2,'xl'=2,'zh'=4,'zl'=2,'core'=2] {'xl','zl','xh'..., dimensions={0} | all-to-all | bytes 2097152 | tf_op jit(solution)/shard_map/all_to_all | solution.py:180
  182.2 4.0 %collective-permute-start.9 = (f32[8,2,32,512]{3,2,1,0:T(8,128)S(1)}, f32[8,2,32,512]{3,2,1,0:T(8,128)S(1)}, u32[]{:S(2)}, u32[]{:S(2)}) collective-permute-start(f32[8,2,32,512]{3,2,1,0:T(8,128)S(1)} %bitcast.39), channel_id=1, source_target_pairs={{0,1},{1,0},{2,3},{3,2},{4,5},{5,4},{6,7},{7,6},{8,9},{9,8},{10,11... | collective-permute-start | bytes 3145736 | tf_op jit(solution)/shard_map/ppermute | solution.py:182
  186.3 2.2 %collective-permute-done.9.theirs = f32[8,2,32,512]{3,2,1,0:T(8,128)S(1)} collective-permute-done((f32[8,2,32,512]{3,2,1,0:T(8,128)S(1)}, f32[8,2,32,512]{3,2,1,0:T(8,128)S(1)}, u32[]{:S(2)}, u32[]{:S(2)}) %collective-permute-start.9) | collective-permute-done | bytes 1048608 | tf_op jit(solution)/shard_map/ppermute | solution.py:182
  188.5 1.2 shard_map.36
  189.7 4.8 %collective-permute-start.10 = (f32[32,512]{1,0:T(8,128)S(1)}, f32[32,512]{1,0:T(8,128)S(1)}, u32[]{:S(2)}, u32[]{:S(2)}) collective-permute-start(f32[32,512]{1,0:T(8,128)S(1)} %shard_map.36), channel_id=1, source_target_pairs={{396,0},{428,1},{398,2},{430,3},{412,4},{444,5},{414,6},{446,7},{3... | collective-permute-start | bytes 196616 | tf_op jit(solution)/shard_map/ppermute | solution.py:35
  194.5 8.9 %collective-permute-done.10 = f32[32,512]{1,0:T(8,128)S(1)} collective-permute-done((f32[32,512]{1,0:T(8,128)S(1)}, f32[32,512]{1,0:T(8,128)S(1)}, u32[]{:S(2)}, u32[]{:S(2)}) %collective-permute-start.10) | collective-permute-done | bytes 65568 | tf_op jit(solution)/shard_map/ppermute | solution.py:35
  (32 shorter events, 5.2 us)
Async XLA Ops:
  0.0 0.9 copy-start
  0.9 16.5 %collective-permute-start.1 = (f32[2,32,512]{2,1,0:T(8,128)S(1)}, f32[2,32,512]{2,1,0:T(8,128)S(1)}, u32[]{:S(2)}, u32[]{:S(2)}) collective-permute-start(f32[2,32,512]{2,1,0:T(8,128)S(1)} %constant_dynamic-update-slice_fusion), channel_id=1, source_target_pairs={{0,0},{1,32},{2,2},{3,34},{4,16},{5,48},{6,18},{7,50},{8,1},{9,33}... | collective-permute-start | bytes 393224 | tf_op jit(solution)/shard_map/ppermute | solution.py:35
  6.9 19.8 %collective-permute-start = (f32[2,32,512]{2,1,0:T(8,128)S(1)}, f32[2,32,512]{2,1,0:T(8,128)S(1)}, u32[]{:S(2)}, u32[]{:S(2)}) collective-permute-start(f32[2,32,512]{2,1,0:T(8,128)S(1)} %constant_dynamic-update-slice_fusion), channel_id=1, source_target_pairs={{0,8},{1,40},{2,10},{3,42},{4,24},{5,56},{6,26},{7,58},{8,9},{9,41... | collective-permute-start | bytes 393224 | tf_op jit(solution)/shard_map/ppermute | solution.py:35
  50.1 4.4 %collective-permute-start.2 = (f32[8,32,896]{2,1,0:T(8,128)S(1)}, f32[8,32,896]{2,1,0:T(8,128)S(1)}, u32[]{:S(2)}, u32[]{:S(2)}) collective-permute-start(f32[8,32,896]{2,1,0:T(8,128)S(1)} %all_to_all.25.mine), channel_id=1, source_target_pairs={{0,1},{1,0},{2,3},{3,2},{4,5},{5,4},{6,7},{7,6},{8,9},{9,8},{10,11... | collective-permute-start | bytes 2752520 | tf_op jit(solution)/shard_map/ppermute | solution.py:165
  55.7 11.3 %collective-permute-start.3 = (f32[2,32,512]{2,1,0:T(8,128)S(1)}, f32[2,32,512]{2,1,0:T(8,128)S(1)}, u32[]{:S(2)}, u32[]{:S(2)}) collective-permute-start(f32[2,32,512]{2,1,0:T(8,128)S(1)} %get-tuple-element.28), channel_id=1, source_target_pairs={{0,128},{32,160},{2,130},{34,162},{16,144},{48,176},{18,146},{50,1... | collective-permute-start | bytes 393224 | tf_op jit(solution)/shard_map/ppermute | solution.py:35
  82.6 6.7 %collective-permute-start.4 = (f32[8,32,896]{2,1,0:T(8,128)S(1)}, f32[8,32,896]{2,1,0:T(8,128)S(1)}, u32[]{:S(2)}, u32[]{:S(2)}) collective-permute-start(f32[8,32,896]{2,1,0:T(8,128)S(1)} %all_to_all.26.mine), channel_id=1, source_target_pairs={{0,1},{1,0},{2,3},{3,2},{4,5},{5,4},{6,7},{7,6},{8,9},{9,8},{10,11... | collective-permute-start | bytes 2752520 | tf_op jit(solution)/shard_map/ppermute | solution.py:165
  90.6 12.8 %collective-permute-start.5 = (f32[2,32,512]{2,1,0:T(8,128)S(1)}, f32[2,32,512]{2,1,0:T(8,128)S(1)}, u32[]{:S(2)}, u32[]{:S(2)}) collective-permute-start(f32[2,32,512]{2,1,0:T(8,128)S(1)} %get-tuple-element.33), channel_id=1, source_target_pairs={{0,256},{32,288},{2,258},{34,290},{16,272},{48,304},{18,274},{50,3... | collective-permute-start | bytes 393224 | tf_op jit(solution)/shard_map/ppermute | solution.py:35
  118.5 7.1 %collective-permute-start.6 = (f32[8,32,896]{2,1,0:T(8,128)S(1)}, f32[8,32,896]{2,1,0:T(8,128)S(1)}, u32[]{:S(2)}, u32[]{:S(2)}) collective-permute-start(f32[8,32,896]{2,1,0:T(8,128)S(1)} %all_to_all.27.mine), channel_id=1, source_target_pairs={{0,1},{1,0},{2,3},{3,2},{4,5},{5,4},{6,7},{7,6},{8,9},{9,8},{10,11... | collective-permute-start | bytes 2752520 | tf_op jit(solution)/shard_map/ppermute | solution.py:165
  126.9 14.6 %collective-permute-start.7 = (f32[2,32,512]{2,1,0:T(8,128)S(1)}, f32[2,32,512]{2,1,0:T(8,128)S(1)}, u32[]{:S(2)}, u32[]{:S(2)}) collective-permute-start(f32[2,32,512]{2,1,0:T(8,128)S(1)} %get-tuple-element.38), channel_id=1, source_target_pairs={{0,4},{32,36},{2,6},{34,38},{16,20},{48,52},{18,22},{50,54},{1,5},... | collective-permute-start | bytes 393224 | tf_op jit(solution)/shard_map/ppermute | solution.py:35
  156.9 6.5 %collective-permute-start.8 = (f32[8,32,896]{2,1,0:T(8,128)S(1)}, f32[8,32,896]{2,1,0:T(8,128)S(1)}, u32[]{:S(2)}, u32[]{:S(2)}) collective-permute-start(f32[8,32,896]{2,1,0:T(8,128)S(1)} %all_to_all.28.mine), channel_id=1, source_target_pairs={{0,1},{1,0},{2,3},{3,2},{4,5},{5,4},{6,7},{7,6},{8,9},{9,8},{10,11... | collective-permute-start | bytes 2752520 | tf_op jit(solution)/shard_map/ppermute | solution.py:165
  182.2 6.3 %collective-permute-start.9 = (f32[8,2,32,512]{3,2,1,0:T(8,128)S(1)}, f32[8,2,32,512]{3,2,1,0:T(8,128)S(1)}, u32[]{:S(2)}, u32[]{:S(2)}) collective-permute-start(f32[8,2,32,512]{3,2,1,0:T(8,128)S(1)} %bitcast.39), channel_id=1, source_target_pairs={{0,1},{1,0},{2,3},{3,2},{4,5},{5,4},{6,7},{7,6},{8,9},{9,8},{10,11... | collective-permute-start | bytes 3145736 | tf_op jit(solution)/shard_map/ppermute | solution.py:182
  189.7 13.7 %collective-permute-start.10 = (f32[32,512]{1,0:T(8,128)S(1)}, f32[32,512]{1,0:T(8,128)S(1)}, u32[]{:S(2)}, u32[]{:S(2)}) collective-permute-start(f32[32,512]{1,0:T(8,128)S(1)} %shard_map.36), channel_id=1, source_target_pairs={{396,0},{428,1},{398,2},{430,3},{412,4},{444,5},{414,6},{446,7},{3... | collective-permute-start | bytes 196616 | tf_op jit(solution)/shard_map/ppermute | solution.py:35

commit v6 on v5

--- a/solution.py
+++ b/solution.py
@@ -75,7 +75,7 @@
     return pieces[0] + pieces[1]
 
 
-def early_kernel(info, mine, later_map, out_left, out_weighted, out_map, turned):
+def early_kernel(info, mine, later_map, out, turned):
     core, column = info[0], info[1]
     left = rows_of_map(column, [lambda at: mine[:, :, at]], turned)
     lefts = [split(left[:, 128 * i : 128 * i + 128]) for i in range(2)]
@@ -86,18 +86,18 @@
         for j in range(3):
             weighted[i + j] += row[:, 128 * j : 128 * j + 128]
     weighted[0] += product(lefts[1], tuple(part[:, 128:256] for part in stored[0]), True)
-    out_left[...] = left
-    out_weighted[...] = jnp.concatenate(weighted, 1)
+    out[:, :256] = left
+    out[:, 256:768] = jnp.concatenate(weighted, 1)
     own = own_first(core, later_map[...])[:, :256]
-    out_map[...] = product(split(own), split(mine[:, :, :512].reshape(256, 512)))
+    out[:, 768:] = product(split(own), split(mine[:, :, :512].reshape(256, 512)))
 
 
-def level_kernel(before_last, info, mine, theirs, term, later_map, early_left, early_weighted, early_map, out, sent, turned, twice):
+def level_kernel(before_last, info, mine, theirs, term, later_map, early, out, sent, turned, twice):
     core, column, counts = info[0], info[1], info[2]
-    left = jnp.concatenate([early_left[...], rows_of_map(column, [lambda at: theirs[:, :, at]], turned)], 1)
+    left = jnp.concatenate([early[:, :256], rows_of_map(column, [lambda at: theirs[:, :, at]], turned)], 1)
     lefts = [split(left[:, 128 * i : 128 * i + 128]) for i in range(4)]
     stored = blocks([theirs], 512, 384)
-    weighted = [early_weighted[:, 128 * i : 128 * i + 128] for i in range(4)]
+    weighted = [early[:, 256 + 128 * i : 384 + 128 * i] for i in range(4)]
     for i in (2, 3):
         row = product(lefts[i], stored[i - 2])
         for j in range(3):
@@ -112,7 +112,7 @@
     total = product(split(own), split(mine[:, :, :512].reshape(256, 512)))
     both = product(split(other), split(theirs[:, :, :512].reshape(256, 512)))
     total = term[...] + jnp.where(counts != 0, total + both[:32], 0.0)
-    new_map = early_map[...] + both[32:]
+    new_map = early[:, 768:] + both[32:]
     if before_last:
         out[...] = total
         sent[...] = jnp.where(info[3] != 0, new_map, total)
@@ -167,7 +167,7 @@
         before_last = level == LEVELS - 2
         info = [core, column, counts, is_earlier]
         early = call(
-            early_kernel, [(32, 256), (32, 512), (32, 512)], [(128, 256)], info, mine, own[0]
+            early_kernel, [(32, 1280)], [(128, 256)], info, mine, own[0]
         )
         both, sent = call(
             functools.partial(level_kernel, before_last),

time: 205 us -> 205 us (level)
  no operation moved by 1% of the time
where the time goes in v6:
time: 205 us; the launch traced here: 204 us
  blocking collectives  86.4 us (42%)
  starting transfers between devices  61.5 us (30%)
  waiting for transfers between devices  43.2 us (21%)
  Pallas kernels  10.1 us (5%)
  local copies, waits for them, and re-layouts  2.14 us (1%)
    all_to_all x4, blocking collectives, local(): lax.all_to_all(jnp.broadcast_to(rows[None], (8, 32, 896)), GROUP, 0, 0, t...  69 us
    ppermute x6, starting transfers between devices, move(): return lax.ppermute(array, AXES, pairs)  41.6 us
    ppermute x6, waiting for transfers between devices, move(): return lax.ppermute(array, AXES, pairs)  36.5 us
    ppermute x5, starting transfers between devices, local(): theirs = lax.ppermute(mine, 'core', [(0, 1), (1, 0)])  20 us
    all_to_all x1, blocking collectives, local(): lax.all_to_all(jnp.broadcast_to(sent[None], (16, 32, 512)), GROUP + ('yl'...  17.4 us
    pallas_call x9, Pallas kernels, call(): pl.pallas_call(kernel, out_shape=[jax.ShapeDtypeStruct(shape, jnp.float32...  10.1 us
    ppermute x5, waiting for transfers between devices, local(): theirs = lax.ppermute(mine, 'core', [(0, 1), (1, 0)])  6.65 us
  transfers between devices with their start and end apart: 11, of which 10 were waited for; matrix products, arithmetic and copies ran while one was open for 0% of the time, Pallas kernels for 2%

profile of v6, /device:TPU:1, one launch (start us, length us, event | category | flops | bytes accessed | tf_op | source)
XLA Modules:
  0.0 204.0 jit_solution(3821266902418852749)
XLA Ops:
  0.9 6.0 %collective-permute-start.1 = (f32[2,32,512]{2,1,0:T(8,128)S(1)}, f32[2,32,512]{2,1,0:T(8,128)S(1)}, u32[]{:S(2)}, u32[]{:S(2)}) collective-permute-start(f32[2,32,512]{2,1,0:T(8,128)S(1)} %constant_dynamic-update-slice_fusion), channel_id=1, source_target_pairs={{0,0},{1,32},{2,2},{3,34},{4,16},{5,48},{6,18},{7,50},{8,1},{9,33}... | collective-permute-start | bytes 393224 | tf_op jit(solution)/shard_map/ppermute | solution.py:35
  6.9 10.4 %collective-permute-start = (f32[2,32,512]{2,1,0:T(8,128)S(1)}, f32[2,32,512]{2,1,0:T(8,128)S(1)}, u32[]{:S(2)}, u32[]{:S(2)}) collective-permute-start(f32[2,32,512]{2,1,0:T(8,128)S(1)} %constant_dynamic-update-slice_fusion), channel_id=1, source_target_pairs={{0,8},{1,40},{2,10},{3,42},{4,24},{5,56},{6,26},{7,58},{8,9},{9,41... | collective-permute-start | bytes 393224 | tf_op jit(solution)/shard_map/ppermute | solution.py:35
  17.5 9.3 %collective-permute-done = f32[2,32,512]{2,1,0:T(8,128)S(1)} collective-permute-done((f32[2,32,512]{2,1,0:T(8,128)S(1)}, f32[2,32,512]{2,1,0:T(8,128)S(1)}, u32[]{:S(2)}, u32[]{:S(2)}) %collective-permute-start) | collective-permute-done | bytes 131104 | tf_op jit(solution)/shard_map/ppermute | solution.py:35
  26.9 23.2 %all_to_all.25.mine = f32[8,32,896]{2,1,0:T(8,128)S(1)} all-to-all(f32[8,32,896]{2,1,0:T(8,128)S(1)} %broadcast_in_dim.12), channel_id=1, replica_groups=mesh['yh'=4,'yl'=2,'xh'=2,'xl'=2,'zh'=4,'zl'=2,'core'=2] {'xl','zl','xh'}, dimensions={0} | all-to-all | bytes 1835008 | tf_op jit(solution)/shard_map/all_to_all | solution.py:164
  50.1 1.9 collective-permute-start.2
  53.1 1.3 collective-permute-done.2.theirs
  54.4 1.3 shard_map.29
  55.7 3.8 %collective-permute-start.3 = (f32[2,32,512]{2,1,0:T(8,128)S(1)}, f32[2,32,512]{2,1,0:T(8,128)S(1)}, u32[]{:S(2)}, u32[]{:S(2)}) collective-permute-start(f32[2,32,512]{2,1,0:T(8,128)S(1)} %get-tuple-element.13), channel_id=1, source_target_pairs={{0,128},{32,160},{2,130},{34,162},{16,144},{48,176},{18,146},{50,1... | collective-permute-start | bytes 393224 | tf_op jit(solution)/shard_map/ppermute | solution.py:35
  59.5 7.5 %collective-permute-done.3 = f32[2,32,512]{2,1,0:T(8,128)S(1)} collective-permute-done((f32[2,32,512]{2,1,0:T(8,128)S(1)}, f32[2,32,512]{2,1,0:T(8,128)S(1)}, u32[]{:S(2)}, u32[]{:S(2)}) %collective-permute-start.3) | collective-permute-done | bytes 131104 | tf_op jit(solution)/shard_map/ppermute | solution.py:35
  67.1 15.5 %all_to_all.26.mine = f32[8,32,896]{2,1,0:T(8,128)S(1)} all-to-all(f32[8,32,896]{2,1,0:T(8,128)S(1)} %broadcast_in_dim.13), channel_id=1, replica_groups=mesh['yh'=4,'yl'=2,'xh'=2,'xl'=2,'zh'=4,'zl'=2,'core'=2] {'xl','zl','xh'}, dimensions={0} | all-to-all | bytes 1835008 | tf_op jit(solution)/shard_map/all_to_all | solution.py:164
  82.6 4.6 %collective-permute-start.4 = (f32[8,32,896]{2,1,0:T(8,128)S(1)}, f32[8,32,896]{2,1,0:T(8,128)S(1)}, u32[]{:S(2)}, u32[]{:S(2)}) collective-permute-start(f32[8,32,896]{2,1,0:T(8,128)S(1)} %all_to_all.26.mine), channel_id=1, source_target_pairs={{0,1},{1,0},{2,3},{3,2},{4,5},{5,4},{6,7},{7,6},{8,9},{9,8},{10,11... | collective-permute-start | bytes 2752520 | tf_op jit(solution)/shard_map/ppermute | solution.py:165
  88.3 1.0 collective-permute-done.4.theirs
  89.3 1.3 shard_map.31
  90.6 7.4 %collective-permute-start.5 = (f32[2,32,512]{2,1,0:T(8,128)S(1)}, f32[2,32,512]{2,1,0:T(8,128)S(1)}, u32[]{:S(2)}, u32[]{:S(2)}) collective-permute-start(f32[2,32,512]{2,1,0:T(8,128)S(1)} %get-tuple-element.15), channel_id=1, source_target_pairs={{0,256},{32,288},{2,258},{34,290},{16,272},{48,304},{18,274},{50,3... | collective-permute-start | bytes 393224 | tf_op jit(solution)/shard_map/ppermute | solution.py:35
  98.0 5.4 %collective-permute-done.5 = f32[2,32,512]{2,1,0:T(8,128)S(1)} collective-permute-done((f32[2,32,512]{2,1,0:T(8,128)S(1)}, f32[2,32,512]{2,1,0:T(8,128)S(1)}, u32[]{:S(2)}, u32[]{:S(2)}) %collective-permute-start.5) | collective-permute-done | bytes 131104 | tf_op jit(solution)/shard_map/ppermute | solution.py:35
  103.5 15.0 %all_to_all.27.mine = f32[8,32,896]{2,1,0:T(8,128)S(1)} all-to-all(f32[8,32,896]{2,1,0:T(8,128)S(1)} %broadcast_in_dim.14), channel_id=1, replica_groups=mesh['yh'=4,'yl'=2,'xh'=2,'xl'=2,'zh'=4,'zl'=2,'core'=2] {'xl','zl','xh'}, dimensions={0} | all-to-all | bytes 1835008 | tf_op jit(solution)/shard_map/all_to_all | solution.py:164
  118.5 5.0 %collective-permute-start.6 = (f32[8,32,896]{2,1,0:T(8,128)S(1)}, f32[8,32,896]{2,1,0:T(8,128)S(1)}, u32[]{:S(2)}, u32[]{:S(2)}) collective-permute-start(f32[8,32,896]{2,1,0:T(8,128)S(1)} %all_to_all.27.mine), channel_id=1, source_target_pairs={{0,1},{1,0},{2,3},{3,2},{4,5},{5,4},{6,7},{7,6},{8,9},{9,8},{10,11... | collective-permute-start | bytes 2752520 | tf_op jit(solution)/shard_map/ppermute | solution.py:165
  124.5 1.1 collective-permute-done.6.theirs
  125.6 1.3 shard_map.33
  126.9 9.2 %collective-permute-start.7 = (f32[2,32,512]{2,1,0:T(8,128)S(1)}, f32[2,32,512]{2,1,0:T(8,128)S(1)}, u32[]{:S(2)}, u32[]{:S(2)}) collective-permute-start(f32[2,32,512]{2,1,0:T(8,128)S(1)} %get-tuple-element.17), channel_id=1, source_target_pairs={{0,4},{32,36},{2,6},{34,38},{16,20},{48,52},{18,22},{50,54},{1,5},... | collective-permute-start | bytes 393224 | tf_op jit(solution)/shard_map/ppermute | solution.py:35
  136.1 5.4 %collective-permute-done.7 = f32[2,32,512]{2,1,0:T(8,128)S(1)} collective-permute-done((f32[2,32,512]{2,1,0:T(8,128)S(1)}, f32[2,32,512]{2,1,0:T(8,128)S(1)}, u32[]{:S(2)}, u32[]{:S(2)}) %collective-permute-start.7) | collective-permute-done | bytes 131104 | tf_op jit(solution)/shard_map/ppermute | solution.py:35
  141.6 15.3 %all_to_all.28.mine = f32[8,32,896]{2,1,0:T(8,128)S(1)} all-to-all(f32[8,32,896]{2,1,0:T(8,128)S(1)} %broadcast_in_dim.15), channel_id=1, replica_groups=mesh['yh'=4,'yl'=2,'xh'=2,'xl'=2,'zh'=4,'zl'=2,'core'=2] {'xl','zl','xh'}, dimensions={0} | all-to-all | bytes 1835008 | tf_op jit(solution)/shard_map/all_to_all | solution.py:164
  156.9 4.4 %collective-permute-start.8 = (f32[8,32,896]{2,1,0:T(8,128)S(1)}, f32[8,32,896]{2,1,0:T(8,128)S(1)}, u32[]{:S(2)}, u32[]{:S(2)}) collective-permute-start(f32[8,32,896]{2,1,0:T(8,128)S(1)} %all_to_all.28.mine), channel_id=1, source_target_pairs={{0,1},{1,0},{2,3},{3,2},{4,5},{5,4},{6,7},{7,6},{8,9},{9,8},{10,11... | collective-permute-start | bytes 2752520 | tf_op jit(solution)/shard_map/ppermute | solution.py:165
  161.4 1.0 shard_map.34.early
  162.3 1.1 collective-permute-done.8.theirs
  163.4 1.3 shard_map.35
  164.8 17.4 %all_to_all.29 = f32[16,32,512]{2,1,0:T(8,128)S(1)} all-to-all(f32[16,32,512]{2,1,0:T(8,128)S(1)} %broadcast_in_dim.16), channel_id=1, replica_groups=mesh['yh'=4,'yl'=2,'xh'=2,'xl'=2,'zh'=4,'zl'=2,'core'=2] {'xl','zl','xh'..., dimensions={0} | all-to-all | bytes 2097152 | tf_op jit(solution)/shard_map/all_to_all | solution.py:180
  182.2 4.0 %collective-permute-start.9 = (f32[8,2,32,512]{3,2,1,0:T(8,128)S(1)}, f32[8,2,32,512]{3,2,1,0:T(8,128)S(1)}, u32[]{:S(2)}, u32[]{:S(2)}) collective-permute-start(f32[8,2,32,512]{3,2,1,0:T(8,128)S(1)} %bitcast.39), channel_id=1, source_target_pairs={{0,1},{1,0},{2,3},{3,2},{4,5},{5,4},{6,7},{7,6},{8,9},{9,8},{10,11... | collective-permute-start | bytes 3145736 | tf_op jit(solution)/shard_map/ppermute | solution.py:182
  186.3 2.2 %collective-permute-done.9.theirs = f32[8,2,32,512]{3,2,1,0:T(8,128)S(1)} collective-permute-done((f32[8,2,32,512]{3,2,1,0:T(8,128)S(1)}, f32[8,2,32,512]{3,2,1,0:T(8,128)S(1)}, u32[]{:S(2)}, u32[]{:S(2)}) %collective-permute-start.9) | collective-permute-done | bytes 1048608 | tf_op jit(solution)/shard_map/ppermute | solution.py:182
  188.5 1.2 shard_map.36
  189.7 4.8 %collective-permute-start.10 = (f32[32,512]{1,0:T(8,128)S(1)}, f32[32,512]{1,0:T(8,128)S(1)}, u32[]{:S(2)}, u32[]{:S(2)}) collective-permute-start(f32[32,512]{1,0:T(8,128)S(1)} %shard_map.36), channel_id=1, source_target_pairs={{396,0},{428,1},{398,2},{430,3},{412,4},{444,5},{414,6},{446,7},{3... | collective-permute-start | bytes 196616 | tf_op jit(solution)/shard_map/ppermute | solution.py:35
  194.5 8.9 %collective-permute-done.10 = f32[32,512]{1,0:T(8,128)S(1)} collective-permute-done((f32[32,512]{1,0:T(8,128)S(1)}, f32[32,512]{1,0:T(8,128)S(1)}, u32[]{:S(2)}, u32[]{:S(2)}) %collective-permute-start.10) | collective-permute-done | bytes 65568 | tf_op jit(solution)/shard_map/ppermute | solution.py:35
  (32 shorter events, 5.2 us)
Async XLA Ops:
  0.0 0.9 copy-start
  0.9 16.5 %collective-permute-start.1 = (f32[2,32,512]{2,1,0:T(8,128)S(1)}, f32[2,32,512]{2,1,0:T(8,128)S(1)}, u32[]{:S(2)}, u32[]{:S(2)}) collective-permute-start(f32[2,32,512]{2,1,0:T(8,128)S(1)} %constant_dynamic-update-slice_fusion), channel_id=1, source_target_pairs={{0,0},{1,32},{2,2},{3,34},{4,16},{5,48},{6,18},{7,50},{8,1},{9,33}... | collective-permute-start | bytes 393224 | tf_op jit(solution)/shard_map/ppermute | solution.py:35
  6.9 19.8 %collective-permute-start = (f32[2,32,512]{2,1,0:T(8,128)S(1)}, f32[2,32,512]{2,1,0:T(8,128)S(1)}, u32[]{:S(2)}, u32[]{:S(2)}) collective-permute-start(f32[2,32,512]{2,1,0:T(8,128)S(1)} %constant_dynamic-update-slice_fusion), channel_id=1, source_target_pairs={{0,8},{1,40},{2,10},{3,42},{4,24},{5,56},{6,26},{7,58},{8,9},{9,41... | collective-permute-start | bytes 393224 | tf_op jit(solution)/shard_map/ppermute | solution.py:35
  50.1 4.4 %collective-permute-start.2 = (f32[8,32,896]{2,1,0:T(8,128)S(1)}, f32[8,32,896]{2,1,0:T(8,128)S(1)}, u32[]{:S(2)}, u32[]{:S(2)}) collective-permute-start(f32[8,32,896]{2,1,0:T(8,128)S(1)} %all_to_all.25.mine), channel_id=1, source_target_pairs={{0,1},{1,0},{2,3},{3,2},{4,5},{5,4},{6,7},{7,6},{8,9},{9,8},{10,11... | collective-permute-start | bytes 2752520 | tf_op jit(solution)/shard_map/ppermute | solution.py:165
  55.7 11.3 %collective-permute-start.3 = (f32[2,32,512]{2,1,0:T(8,128)S(1)}, f32[2,32,512]{2,1,0:T(8,128)S(1)}, u32[]{:S(2)}, u32[]{:S(2)}) collective-permute-start(f32[2,32,512]{2,1,0:T(8,128)S(1)} %get-tuple-element.13), channel_id=1, source_target_pairs={{0,128},{32,160},{2,130},{34,162},{16,144},{48,176},{18,146},{50,1... | collective-permute-start | bytes 393224 | tf_op jit(solution)/shard_map/ppermute | solution.py:35
  82.6 6.7 %collective-permute-start.4 = (f32[8,32,896]{2,1,0:T(8,128)S(1)}, f32[8,32,896]{2,1,0:T(8,128)S(1)}, u32[]{:S(2)}, u32[]{:S(2)}) collective-permute-start(f32[8,32,896]{2,1,0:T(8,128)S(1)} %all_to_all.26.mine), channel_id=1, source_target_pairs={{0,1},{1,0},{2,3},{3,2},{4,5},{5,4},{6,7},{7,6},{8,9},{9,8},{10,11... | collective-permute-start | bytes 2752520 | tf_op jit(solution)/shard_map/ppermute | solution.py:165
  90.6 12.8 %collective-permute-start.5 = (f32[2,32,512]{2,1,0:T(8,128)S(1)}, f32[2,32,512]{2,1,0:T(8,128)S(1)}, u32[]{:S(2)}, u32[]{:S(2)}) collective-permute-start(f32[2,32,512]{2,1,0:T(8,128)S(1)} %get-tuple-element.15), channel_id=1, source_target_pairs={{0,256},{32,288},{2,258},{34,290},{16,272},{48,304},{18,274},{50,3... | collective-permute-start | bytes 393224 | tf_op jit(solution)/shard_map/ppermute | solution.py:35
  118.5 7.1 %collective-permute-start.6 = (f32[8,32,896]{2,1,0:T(8,128)S(1)}, f32[8,32,896]{2,1,0:T(8,128)S(1)}, u32[]{:S(2)}, u32[]{:S(2)}) collective-permute-start(f32[8,32,896]{2,1,0:T(8,128)S(1)} %all_to_all.27.mine), channel_id=1, source_target_pairs={{0,1},{1,0},{2,3},{3,2},{4,5},{5,4},{6,7},{7,6},{8,9},{9,8},{10,11... | collective-permute-start | bytes 2752520 | tf_op jit(solution)/shard_map/ppermute | solution.py:165
  126.9 14.6 %collective-permute-start.7 = (f32[2,32,512]{2,1,0:T(8,128)S(1)}, f32[2,32,512]{2,1,0:T(8,128)S(1)}, u32[]{:S(2)}, u32[]{:S(2)}) collective-permute-start(f32[2,32,512]{2,1,0:T(8,128)S(1)} %get-tuple-element.17), channel_id=1, source_target_pairs={{0,4},{32,36},{2,6},{34,38},{16,20},{48,52},{18,22},{50,54},{1,5},... | collective-permute-start | bytes 393224 | tf_op jit(solution)/shard_map/ppermute | solution.py:35
  156.9 6.5 %collective-permute-start.8 = (f32[8,32,896]{2,1,0:T(8,128)S(1)}, f32[8,32,896]{2,1,0:T(8,128)S(1)}, u32[]{:S(2)}, u32[]{:S(2)}) collective-permute-start(f32[8,32,896]{2,1,0:T(8,128)S(1)} %all_to_all.28.mine), channel_id=1, source_target_pairs={{0,1},{1,0},{2,3},{3,2},{4,5},{5,4},{6,7},{7,6},{8,9},{9,8},{10,11... | collective-permute-start | bytes 2752520 | tf_op jit(solution)/shard_map/ppermute | solution.py:165
  182.2 6.3 %collective-permute-start.9 = (f32[8,2,32,512]{3,2,1,0:T(8,128)S(1)}, f32[8,2,32,512]{3,2,1,0:T(8,128)S(1)}, u32[]{:S(2)}, u32[]{:S(2)}) collective-permute-start(f32[8,2,32,512]{3,2,1,0:T(8,128)S(1)} %bitcast.39), channel_id=1, source_target_pairs={{0,1},{1,0},{2,3},{3,2},{4,5},{5,4},{6,7},{7,6},{8,9},{9,8},{10,11... | collective-permute-start | bytes 3145736 | tf_op jit(solution)/shard_map/ppermute | solution.py:182
  189.7 13.7 %collective-permute-start.10 = (f32[32,512]{1,0:T(8,128)S(1)}, f32[32,512]{1,0:T(8,128)S(1)}, u32[]{:S(2)}, u32[]{:S(2)}) collective-permute-start(f32[32,512]{1,0:T(8,128)S(1)} %shard_map.36), channel_id=1, source_target_pairs={{396,0},{428,1},{398,2},{430,3},{412,4},{444,5},{414,6},{446,7},{3... | collective-permute-start | bytes 196616 | tf_op jit(solution)/shard_map/ppermute | solution.py:35
